TPU v7x, 256 devices: a whole 4x4x8 slice. The times are simulated.
256 devices in a mesh: dom: 64 (over x, z, core), mp: 4 (over y).
Axes of the slice: x: 4, y: 4, z: 8, core: 2. Of those that a mesh axis runs over, the one named last changes fastest.
Arguments:
- features: bfloat16 [32768, 1024], P('dom'), may hold values from -16 to 16
- history: float32 [32768, 1024], P('dom'), may hold values from -6 to 6
- weights: bfloat16 [1024, 5, 1024], P(None, None, 'mp'), may hold values from -0.1875 to 0.1875
- cotangent: bfloat16 [32768, 1024], P('dom', 'mp'), may hold values from -6 to 6
- send_rows: int32 [64, 64, 8], P('dom'), may hold values from 0 to 1023
- neighbors: int32 [4, 32768, 8], P(None, 'dom'), may hold values from 0 to 1023
Outputs:
- output: bfloat16 [32768, 1024], P('dom', 'mp')
- grad_features: bfloat16 [32768, 1024], P('dom', 'mp')
- grad_weights: float32 [1024, 5, 1024], P('dom', None, 'mp')
All inputs are finite; a program needn't handle non-finite values.
Results may differ from a plain program's by a relative error of at most 0.0052.
Values may be sent and summed in bfloat16 or wider, within the bound.
A program may use at most 128 MiB of HBM per device.

v0:
```python
import jax
import jax.numpy as jnp
from jax import lax
from jax.sharding import PartitionSpec as P


def silu_slope(value):
    sigma = jax.nn.sigmoid(value)
    return sigma * (1.0 + value * (1.0 - sigma))


def one_hot_rows(indices, columns):
    positions = lax.broadcasted_iota(jnp.int32, (1, columns), 1)
    return (indices[:, None] == positions).astype(jnp.float32)


def neighbor_counts(nbr_rel, columns, fanout):
    positions = lax.broadcasted_iota(jnp.int32, (1, columns), 1)
    total = jnp.zeros((nbr_rel.shape[0], columns), jnp.float32)
    for k in range(fanout):
        total = total + (nbr_rel[:, k : k + 1] == positions).astype(jnp.float32)
    return total


def pick_rows(source, chosen):
    selector = one_hot_rows(chosen.reshape(-1), source.shape[0]).astype(jnp.bfloat16)
    picked = jnp.dot(selector, source, preferred_element_type=jnp.float32).astype(jnp.bfloat16)
    return picked.reshape(chosen.shape[0], chosen.shape[1], source.shape[1])


def spread_rows(per_relation, counts, table_rows, fanout):
    rows = per_relation.shape[1]
    width = per_relation.shape[2]
    relations = counts.shape[0]
    stacked_counts = counts.reshape(relations * rows, table_rows)
    scaled = (per_relation[:relations] / fanout).reshape(relations * rows, width)
    grad_table = lax.dot_general(
        stacked_counts,
        scaled,
        (((0,), (0,)), ((), ())),
        precision=lax.Precision.HIGHEST,
        preferred_element_type=jnp.float32,
    )
    own_part = jnp.concatenate(
        [per_relation[relations], jnp.zeros((table_rows - rows, width), jnp.float32)], axis=0
    )
    return grad_table + own_part


def shards(features, history, weights, cotangent, send_rows, neighbors):
    rows, width = features.shape
    fanout = neighbors.shape[2]
    relations = neighbors.shape[0]
    peer_count = lax.axis_size("dom")
    slots = send_rows.shape[2]
    groups = lax.axis_size("mp")
    part = width // groups
    source = jnp.concatenate([features, history.astype(jnp.bfloat16)], axis=0)
    chosen = send_rows[0]
    picked = pick_rows(source, chosen)
    halo = lax.all_to_all(picked, "dom", split_axis=0, concat_axis=0, tiled=True)
    table = jnp.concatenate([features, halo.reshape(peer_count * slots, width)], axis=0)
    table_rows = rows + peer_count * slots
    counts = jnp.stack(
        [neighbor_counts(neighbors[r], table_rows, fanout) for r in range(relations)]
    )
    counts_low = counts.astype(jnp.bfloat16)
    aggs = [
        (jnp.dot(counts_low[r], table, preferred_element_type=jnp.float32) / fanout).astype(
            jnp.bfloat16
        )
        for r in range(relations)
    ]
    stack = jnp.stack(aggs + [features])
    pre = jnp.einsum("rnd,dro->no", stack, weights, preferred_element_type=jnp.float32)
    output = jax.nn.silu(pre).astype(jnp.bfloat16)
    dpre = (cotangent.astype(jnp.float32) * silu_slope(pre)).astype(jnp.bfloat16)
    back = jnp.einsum("no,dro->rnd", dpre, weights, preferred_element_type=jnp.float32)
    partial_table = spread_rows(back, counts, table_rows, fanout)
    grad_table = lax.psum_scatter(partial_table, "mp", scatter_dimension=1, tiled=True)
    halo_grad = grad_table[rows:].reshape(peer_count, slots, part).astype(jnp.bfloat16)
    returned = lax.all_to_all(halo_grad, "dom", split_axis=0, concat_axis=0, tiled=True)
    owner_map = one_hot_rows(chosen.reshape(peer_count * slots), rows)
    added = lax.dot_general(
        owner_map,
        returned.reshape(peer_count * slots, part).astype(jnp.float32),
        (((0,), (0,)), ((), ())),
        precision=lax.Precision.HIGHEST,
        preferred_element_type=jnp.float32,
    )
    grad_features = (grad_table[:rows] + added).astype(jnp.bfloat16)
    grad_weights = lax.psum_scatter(
        jnp.einsum("rnd,no->dro", stack, dpre, preferred_element_type=jnp.float32),
        "dom",
        scatter_dimension=0,
        tiled=True,
    )
    return (output, grad_features, grad_weights)


def solution(mesh):
    in_specs = (
        P("dom", None),
        P("dom", None),
        P(None, None, "mp"),
        P("dom", "mp"),
        P("dom", None, None),
        P(None, "dom", None),
    )
    out_specs = (P("dom", "mp"), P("dom", "mp"), P("dom", None, "mp"))
    return jax.shard_map(shards, mesh=mesh, in_specs=in_specs, out_specs=out_specs, check_vma=False)
```

profile of v0, /device:TPU:1, one launch (start us, length us, event | category | flops | bytes accessed | tf_op | source)
XLA Modules:
  0.0 307.6 jit_solution(17380536624806766211)
XLA Ops:
  7.2 0.9 copy.14
  8.2 1.8 convert_element_type.400
  10.1 2.3 fusion.6
  12.4 13.3 %all-to-all-start = ((bf16[64,8,1024]{2,1,0:T(8,128)(2,1)}), bf16[64,8,1024]{2,1,0:T(8,128)(2,1)}, u32[]{:S(2)}, u32[]{:S(2)}) async-start(bf16[64,8,1024]{2,1,0:T(8,128)(2,1)} %fusion.6), calls=%async_computation | async-start | bytes 2097152 | tf_op jit(solution)/shard_map/all_to_all | solution.py:61
  25.8 1.9 convert_add_fusion.1
  27.7 1.9 convert_add_fusion.3
  29.6 1.9 convert_add_fusion
  31.6 1.9 convert_add_fusion.2
  33.5 1.4 copy-done.7
  34.9 2.4 fusion.1
  37.3 16.9 %all-to-all-done = bf16[64,8,1024]{2,1,0:T(8,128)(2,1)} async-done(((bf16[64,8,1024]{2,1,0:T(8,128)(2,1)}), bf16[64,8,1024]{2,1,0:T(8,128)(2,1)}, u32[]{:S(2)}, u32[]{:S(2)}) %all-to-all-start) | async-done | bytes 1048608 | tf_op jit(solution)/shard_map/all_to_all | solution.py:61
  54.1 3.3 %fusion.8 = bf16[5,512,1024]{2,1,0:T(8,128)(2,1)S(1)} fusion(bf16[4,512,1024]{1,2,0:T(8,128)(2,1)} %fusion.1, bf16[512,1024]{1,0:T(8,128)(2,1)} %param.6, bf16[512,1024]{1,0:T(8,128)(2,1)} %bitcast.38), kind=kOutput, calls=%fused_computation.58 | convolution fusion | flops 1078984704 | bytes 4194304 | tf_op jit(solution)/shard_map/dot_general | solution.py:69
  57.4 0.1 copy-done.13
  57.6 2.5 fusion.10
  60.1 2.5 fusion.12
  62.6 2.5 fusion.14
  65.2 2.4 multiply_convert_fusion.5
  67.6 1.6 convolution_bitcast_fusion
  69.2 0.2 slice_bitcast_fusion
  69.5 0.3 copy-done.8
  69.8 1.1 copy-done.2
  70.9 0.6 copy-done.4
  71.6 27.6 %bitcast_add_fusion = f32[1024,1024]{1,0:T(8,128)} fusion(f32[512,1024]{1,0:T(8,128)S(1)} %slice_bitcast_fusion, f32[5,512,1024]{2,1,0:T(8,128)S(1)} %convolution_bitcast_fusion, f32[1,512,1024]{1,2,0:T(8,128)S(1)} %copy-done.6, f32[1,512,1024]{1,2,0:T(8,128)S(1)} %copy-done.2, f32[1,512,1024]{1,2,0:T(8,128)S(1)} %copy-done.8, f32[1,512,1024]{1,2,0:T(8,128)S(1)} %copy-done.4), kind=kOutput, calls=%fused_computation.4 | convolution fusion | flops 25779240960 | bytes 23068672 | tf_op jit(solution)/shard_map/dot_general | solution.py:37
  99.2 0.3 reduce-scatter.5.cloned.1.call-start
  99.5 6.6 %convolution_bitcast_fusion.1 = f32[1024,5,256]{0,2,1:T(8,128)} fusion(bf16[5,512,1024]{2,1,0:T(8,128)(2,1)} %copy-done.9, f32[512,256]{1,0:T(8,128)S(1)} %get-tuple-element.49, bf16[512,256]{1,0:T(8,128)(2,1)S(1)} %copy-done.11), kind=kOutput, calls=%fused_computation.7 | convolution fusion | flops 1343488000 | bytes 11272192 | tf_op jit(solution)/shard_map/rnd,no->dro/dot_general | solution.py:93
  106.1 8.2 %copy.16 = f32[1024,5,256]{2,1,0:T(8,128)} copy(f32[1024,5,256]{0,2,1:T(8,128)} %convolution_bitcast_fusion.1) | data formatting | bytes 10485760 | tf_op jit(solution)/shard_map/rnd,no->dro/transpose | solution.py:93
  114.3 31.5 %reduce-scatter.3.cloned.1.call-done = f32[1024,256]{1,0:T(8,128)} async-done(((f32[1024,1024]{1,0:T(8,128)}), f32[1024,256]{1,0:T(8,128)}) %reduce-scatter.3.cloned.1.call-update) | async-done | bytes 1048592 | tf_op jit(solution)/shard_map/reduce_scatter | solution.py:80
  145.8 1.8 fusion.18
  147.6 10.6 %all-to-all-start.1 = ((bf16[64,8,256]{2,1,0:T(8,128)(2,1)}), bf16[64,8,256]{2,1,0:T(8,128)(2,1)S(1)}, u32[]{:S(2)}, u32[]{:S(2)}) async-start(bf16[64,8,256]{2,1,0:T(8,128)(2,1)} %fusion.18), calls=%async_computation.2 | async-start | bytes 524288 | tf_op jit(solution)/shard_map/all_to_all | solution.py:82
  158.2 138.7 %reduce-scatter.5.cloned.1.call-done = f32[16,5,256]{2,1,0:T(8,128)} async-done(((f32[1024,5,256]{2,1,0:T(8,128)}), f32[16,5,256]{2,1,0:T(8,128)}) %reduce-scatter.5.cloned.1.call-update) | async-done | bytes 81936 | tf_op jit(solution)/shard_map/reduce_scatter | solution.py:92
  296.9 1.6 copy.17
  298.5 2.3 fusion.15
  (34 shorter events, 0.4 us)
Async XLA Ops:
  7.2 58.0 %copy-start = (bf16[1024,5,256]{2,0,1:T(8,128)(2,1)S(1)}, bf16[1024,5,256]{2,0,1:T(8,128)(2,1)}, u32[]{:S(2)}) copy-start(bf16[1024,5,256]{2,0,1:T(8,128)(2,1)} %param.8) | copy-start | bytes 7864324
  8.2 1.9 copy-start.12
  12.4 13.4 %copy-start.14 = (s32[4,512,8]{1,2,0:T(8,128)S(1)}, s32[4,512,8]{1,2,0:T(8,128)}, u32[]{:S(2)}) copy-start(s32[4,512,8]{1,2,0:T(8,128)} %param.11) | copy-start | bytes 196612
  12.4 41.8 %all-to-all-start = ((bf16[64,8,1024]{2,1,0:T(8,128)(2,1)}), bf16[64,8,1024]{2,1,0:T(8,128)(2,1)}, u32[]{:S(2)}, u32[]{:S(2)}) async-start(bf16[64,8,1024]{2,1,0:T(8,128)(2,1)} %fusion.6), calls=%async_computation | async-start | bytes 2097152 | tf_op jit(solution)/shard_map/all_to_all | solution.py:61
  25.7 120.2 %reduce-scatter.3.cloned.1.call-start = ((), (), s32[]{:S(2)}) async-start(), calls=%async_computation.4 | async-start | bytes 5242880 | tf_op jit(solution)/shard_map/reduce_scatter | solution.py:80
  27.7 5.7 %copy-start.1 = (f32[1,512,1024]{1,2,0:T(8,128)}, f32[1,512,1024]{1,2,0:T(8,128)S(1)}, u32[]{:S(2)}) copy-start(f32[1,512,1024]{1,2,0:T(8,128)S(1)} %convert_add_fusion.1) | copy-start | bytes 6291460
  29.6 3.8 %copy-start.3 = (f32[1,512,1024]{1,2,0:T(8,128)}, f32[1,512,1024]{1,2,0:T(8,128)S(1)}, u32[]{:S(2)}) copy-start(f32[1,512,1024]{1,2,0:T(8,128)S(1)} %convert_add_fusion.3) | copy-start | bytes 6291460
  31.5 1.9 copy-start.5
  33.5 1.4 copy-start.7
  54.1 3.3 %copy-start.10 = (bf16[4,512,1024]{1,2,0:T(8,128)(2,1)S(1)}, bf16[4,512,1024]{1,2,0:T(8,128)(2,1)}, u32[]{:S(2)}) copy-start(bf16[4,512,1024]{1,2,0:T(8,128)(2,1)} %fusion.1) | copy-start | bytes 12582916
  54.1 3.4 %copy-start.13 = (bf16[512,1024]{1,0:T(8,128)(2,1)S(1)}, bf16[512,1024]{1,0:T(8,128)(2,1)}, u32[]{:S(2)}) copy-start(bf16[512,1024]{1,0:T(8,128)(2,1)} %param.6) | copy-start | bytes 3145732
  65.2 2.4 copy-start.9
  65.2 2.4 copy-start.11
  67.6 1.9 copy-start.6
  67.6 2.2 copy-start.8
  69.2 1.7 copy-start.2
  69.2 2.4 copy-start.4
  99.2 197.7 %reduce-scatter.5.cloned.1.call-start = ((), (), s32[]{:S(2)}) async-start(), calls=%async_computation.5 | async-start | bytes 8519680 | tf_op jit(solution)/shard_map/reduce_scatter | solution.py:92
  147.6 150.9 %all-to-all-start.1 = ((bf16[64,8,256]{2,1,0:T(8,128)(2,1)}), bf16[64,8,256]{2,1,0:T(8,128)(2,1)S(1)}, u32[]{:S(2)}, u32[]{:S(2)}) async-start(bf16[64,8,256]{2,1,0:T(8,128)(2,1)} %fusion.18), calls=%async_computation.2 | async-start | bytes 524288 | tf_op jit(solution)/shard_map/all_to_all | solution.py:82
Sparse Core Ops, SparseCore 0:
  99.4 46.4 reduce-scatter.2
  150.6 146.2 reduce-scatter.4
where the time goes:
time: 312 us; the launch traced here: 308 us
  waiting for transfers between devices  187 us (60%)
  matrix products  53.6 us (17%)
  starting transfers between devices  24.3 us (8%)
  local copies, waits for them, and re-layouts  16.6 us (5%)
  between operations  14.3 us (5%)
  other arithmetic  11.8 us (4%)
    reduce_scatter x1, waiting for transfers between devices, shards(): lax.psum_scatter(jnp.einsum('rnd,no->dro', stack, dpre, preferred_element...  139 us
    reduce_scatter x1, waiting for transfers between devices, shards(): lax.psum_scatter(partial_table, 'mp', scatter_dimension=1, tiled=True)  31.5 us
    dot_general x1, matrix products, spread_rows(): lax.dot_general(stacked_counts, scaled, (((0,), (0,)), ((), ())), precisi...  27.6 us
    all_to_all x1, waiting for transfers between devices, shards(): lax.all_to_all(picked, 'dom', split_axis=0, concat_axis=0, tiled=True)  16.9 us
    all_to_all x1, starting transfers between devices, shards(): lax.all_to_all(picked, 'dom', split_axis=0, concat_axis=0, tiled=True)  13.3 us
    dot_general x4, matrix products, shards(): jnp.dot(counts_low[r], table, preferred_element_type=jnp.float32) / fanout  10.7 us
    all_to_all x1, starting transfers between devices, shards(): lax.all_to_all(halo_grad, 'dom', split_axis=0, concat_axis=0, tiled=True)  10.6 us
    transpose x1, local copies, waits for them, and re-layouts, shards(): jnp.einsum('rnd,no->dro', stack, dpre, preferred_element_type=jnp.float32)  8.18 us
  transfers between devices with their start and end apart: 4, of which 3 were waited for; matrix products, arithmetic and copies ran while one was open for 9% of the time, Pallas kernels for 0%

commit v1 on v0

v1 whole, which is shorter than its diff:
```python
import functools

import jax
import jax.numpy as jnp
from jax import lax
from jax.experimental import pallas as pl
from jax.experimental.pallas import tpu as pltpu
from jax.sharding import PartitionSpec as P

MESH = pl.DeviceIdType.MESH
CORES = 2
F32 = jnp.float32
BF16 = jnp.bfloat16


def dot(a, b):
    return jnp.dot(a, b, preferred_element_type=F32)


def dot_nt(a, b):
    return lax.dot_general(a, b, (((1,), (1,)), ((), ())), preferred_element_type=F32)


def loop(count, body):
    lax.fori_loop(0, count, lambda i, c: (body(i), c)[1], 0)


def kernel(
    X, Z, Y,
    feat, hist, w, cot, sendcol, sendrow, nbr,
    out, gf, gw,
    histv, src, asib, aown, arecv, slabs, halo, wd, nbrcol, cnt, tab, tacc, pre, tabT,
    dp, dT, eT, gsend, gown, grecv, gx, rx, gz, gzs, rz, bT, gtT, hg, ret, rets,
    hist_sem, sib_sem, halo_sem, w_sem, wf_sem, ag1_sem, ag2_sem, gc_sem, gx_sem, gz_sem, ret_sem, rsib_sem,
):
    N, D = feat.shape
    R = nbr.shape[0]
    K = nbr.shape[1]
    O = w.shape[2]
    S = D // Y
    CH = X * Z
    HR = halo.shape[1]
    SL = HR // CH
    T = N + HR
    GR = gw.shape[1]

    dom = lax.axis_index("dom")
    y = lax.axis_index("mp")
    c = lax.rem(dom, CORES)
    q = dom // CORES
    z = lax.rem(q, Z)
    x = q // Z

    def at(chip, core, yy):
        return {"dom": chip * CORES + core, "mp": yy}

    def ring(v, size):
        return lax.rem(v + size, size)

    def remote(s, d, ss, rs, dev):
        return pltpu.make_async_remote_copy(
            src_ref=s, dst_ref=d, send_sem=ss, recv_sem=rs, device_id=dev, device_id_type=MESH
        )

    sibling = at(q, 1 - c, y)
    up, down, far = ring(y + 1, Y), ring(y - 1, Y), ring(y + 2, Y)

    hist_copy = pltpu.make_async_copy(hist.at[:, pl.ds(pl.multiple_of(y * S, 128), S)], histv, hist_sem)
    hist_copy.start()

    barrier = pltpu.get_barrier_semaphore()

    def greet(dev):
        pl.semaphore_signal(barrier, inc=1, device_id=dev, device_id_type=MESH)

    greet(sibling)
    for k in range(1, Y):
        greet(at(q, c, ring(y + k, Y)))
    loop(CH - 1, lambda i: greet(at(lax.rem(q + 1 + i, CH), c, y)))

    src[0:N, :] = feat[:, pl.ds(pl.multiple_of(y * S, 128), S)]
    hist_copy.wait()
    src[N : 2 * N, :] = histv[...].astype(BF16)

    def pick(k, dst):
        step = min(128, HR)

        def body(i):
            rows = pl.ds(pl.multiple_of(i * step, step), step)
            col = sendcol[k, rows, :]
            sel = jnp.where(col == lax.broadcasted_iota(jnp.int32, (step, 2 * N), 1), 1.0, 0.0).astype(BF16)
            dst[rows, :] = dot(sel, src[...]).astype(BF16)

        loop(HR // step, body)

    pick(1, asib)
    pl.semaphore_wait(barrier, CH + Y - 1)
    sib_copy = remote(asib, arecv, sib_sem.at[0], sib_sem.at[1], sibling)
    sib_copy.start()
    pick(0, aown)
    sib_copy.wait_recv()
    slabs[...] = aown[...] + arecv[...]
    mine = pl.ds(pl.multiple_of(q * SL, SL), SL)
    halo[y, mine, :] = slabs[mine, :]

    def chip_rows(i):
        chip = lax.rem(q + 1 + i, CH)
        return chip, pl.ds(pl.multiple_of(chip * SL, SL), SL)

    def send_slab(i):
        chip, rows = chip_rows(i)
        remote(slabs.at[rows, :], halo.at[y, mine, :], halo_sem.at[0], halo_sem.at[1], at(chip, c, y)).start()

    loop(CH - 1, send_slab)
    others = pl.ds(0, HR - SL)
    halo_all = remote(slabs.at[others, :], halo.at[y, others, :], halo_sem.at[0], halo_sem.at[1], sibling)

    half = S // CORES
    w_copies = []
    for k in range(1, Y):
        to = ring(y + k, Y)
        cp = remote(
            w.at[:, pl.ds(pl.multiple_of(to * S + c * half, half), half), :],
            wd.at[y, :, pl.ds(pl.multiple_of(c * half, half), half), :],
            w_sem.at[0, k], w_sem.at[1, k], at(q, c, to),
        )
        cp.start()
        w_copies.append(cp)

    def counts(r):
        nbrcol[r] = jnp.transpose(nbr[r], (1, 0))
        step = min(32, N)

        def body(i):
            rows = pl.ds(pl.multiple_of(i * step, step), step)
            cols = nbrcol[r, rows, :]
            pos = lax.broadcasted_iota(jnp.int32, (step, T), 1)
            total = jnp.zeros((step, T), F32)
            for k in range(K):
                total = total + jnp.where(cols[:, k : k + 1] == pos, 1.0 / K, 0.0)
            cnt[r, rows, :] = total.astype(BF16)

        loop(N // step, body)

    loop(R, counts)

    def local_tab(r):
        tab[r, 0:N, :] = dot(feat[...], w[r]).astype(BF16)

    loop(R, local_tab)

    def gather_start(buf, sem):
        m = buf.shape[1] // 2
        lo, hi = pl.ds(0, m), pl.ds(m, m)
        dev_up, dev_down = at(q, c, up), at(q, c, down)

        def cp(slot, rows, k, dev):
            return remote(buf.at[slot, rows, :], buf.at[slot, rows, :], sem.at[0, k], sem.at[1, k], dev)

        copies = [
            cp(y, lo, 0, dev_up), cp(y, hi, 1, dev_down), cp(y, hi, 2, dev_up), cp(y, lo, 3, dev_down),
            cp(down, lo, 4, dev_up), cp(up, hi, 5, dev_down),
        ]
        for one in copies[:4]:
            one.start()
        return copies

    def gather_forward(copies):
        copies[0].wait_recv()
        copies[4].start()
        copies[1].wait_recv()
        copies[5].start()

    halo_all.wait_recv()
    ag1 = gather_start(halo, ag1_sem)

    pre[...] = dot(feat[...], w[R])

    def local_pre(r):
        pre[...] += dot(cnt[r, :, 0:N], tab[r, 0:N, :])

    loop(R, local_pre)
    gather_forward(ag1)

    def add_tab(slot, first):
        rows = pl.ds(pl.multiple_of(slot * S, S), S)

        def body(r):
            part = dot(halo[slot], w[r, rows, :])
            if first:
                tacc[r] = part
            else:
                tacc[r] += part

        loop(R, body)

    def turn_halo(slot):
        tabT[pl.ds(pl.multiple_of(slot * S, S), S), N:T] = jnp.transpose(halo[slot], (1, 0))

    add_tab(y, True)
    tabT[:, 0:N] = jnp.transpose(feat[...], (1, 0))
    turn_halo(y)
    ag1[2].wait_recv()
    add_tab(down, False)
    turn_halo(down)
    ag1[3].wait_recv()
    add_tab(up, False)
    turn_halo(up)
    ag1[4].wait_recv()
    ag1[5].wait_recv()
    far_rows = pl.ds(pl.multiple_of(far * S, S), S)

    def halo_pre(r):
        tab[r, N:T, :] = (tacc[r] + dot(halo[far], w[r, far_rows, :])).astype(BF16)
        pre[...] += dot(cnt[r, :, N:T], tab[r, N:T, :])

    loop(R, halo_pre)

    v = pre[...]
    s = 1.0 / (1.0 + jnp.exp(-v))
    out[...] = (v * s).astype(BF16)
    slope = (cot[...].astype(F32) * (s * (1.0 + v * (1.0 - s)))).astype(BF16)
    dp[y] = slope
    ag2 = gather_start(dp, ag2_sem)
    dT[...] = jnp.transpose(slope, (1, 0))
    turn_halo(far)

    w_forwards = []
    for k in range(1, Y):
        frm = ring(y - k, Y)
        w_copies[k - 1].wait_recv()
        part = wd.at[frm, :, pl.ds(pl.multiple_of(c * half, half), half), :]
        cp = remote(part, part, wf_sem.at[0, k], wf_sem.at[1, k], sibling)
        cp.start()
        w_forwards.append(cp)
    wd[y] = w[:, pl.ds(pl.multiple_of(y * S, S), S), :]

    def spread_units(r):
        eT[r] = dot(dT[...], cnt[r]).astype(BF16)

    loop(R, spread_units)
    gather_forward(ag2)
    tile = min(8, CH)
    span = tile * CORES * GR

    def core_copy(r):
        return remote(gsend.at[r], grecv.at[r], gc_sem.at[0, r], gc_sem.at[1, r], sibling)

    def put_terms(r, i, part):
        part = part.reshape(tile, CORES, GR, O)
        chips = pl.ds(pl.multiple_of(i * tile, tile), tile)
        gown[r, chips] = jnp.where(c == 0, part[:, 0], part[:, 1])
        gsend[r, chips] = jnp.where(c == 0, part[:, 1], part[:, 0]).astype(BF16)

    def terms(r):
        def body(i):
            rows = pl.ds(pl.multiple_of(i * span, span), span)
            put_terms(r, i, dot_nt(tabT[rows, :], eT[r]))

        loop(CH // tile, body)
        core_copy(r).start()

    loop(R, terms)

    def own_terms(i):
        rows = pl.ds(pl.multiple_of(i * span, span), span)
        put_terms(R, i, dot(tabT[rows, 0:N], dp[y]))

    loop(CH // tile, own_terms)
    core_copy(R).start()

    def x_copy(r, k):
        to = ring(x + k, X)
        return remote(
            gx.at[r, pl.ds(to * Z, Z)], rx.at[r, k - 1], gx_sem.at[0, r, k], gx_sem.at[1, r, k], at(to * Z + z, c, y)
        )

    def along_x(r):
        core_copy(r).wait_recv()

        def body(i):
            chips = pl.ds(i * tile, tile)
            total = gown[r, chips] + grecv[r, chips].astype(F32)
            gown[r, chips] = total
            gx[r, chips] = total.astype(BF16)

        loop(CH // tile, body)
        for k in range(1, X):
            x_copy(r, k).start()

    loop(R + 1, along_x)

    for k in (2, 3, 4, 5):
        ag2[k].wait_recv()
    for one in w_forwards:
        one.wait_recv()

    def back(r):
        total = dot_nt(wd[0, r], dp[0])
        for k in range(1, Y):
            total = total + dot_nt(wd[k, r], dp[k])
        return total

    def put_back(r):
        bT[r] = back(r).astype(BF16)

    loop(R, put_back)
    gtT[:, 0:N] = back(R)
    gtT[:, N:T] = dot(bT[0], cnt[0, :, N:T])
    gtT[:, 0:N] += dot(bT[0], cnt[0, :, 0:N])

    def add_table(r):
        gtT[...] += dot(bT[r + 1], cnt[r + 1])

    loop(R - 1, add_table)

    hg[...] = jnp.transpose(gtT[:, N:T], (1, 0)).astype(BF16)
    ret[mine, :] = hg[mine, :]

    def return_slab(i):
        chip, rows = chip_rows(i)
        remote(hg.at[rows, :], ret.at[mine, :], ret_sem.at[0], ret_sem.at[1], at(chip, c, y)).start()

    loop(CH - 1, return_slab)
    ret_all = remote(hg.at[others, :], ret.at[others, :], ret_sem.at[0], ret_sem.at[1], sibling)

    def z_copy(k):
        to = ring(z + k, Z)
        return remote(gzs.at[:, to], rz.at[k - 1], gz_sem.at[0, k], gz_sem.at[1, k], at(x * Z + to, c, y))

    def along_z(r):
        total = gown[r, pl.ds(x * Z, Z)]
        for k in range(1, X):
            x_copy(r, k).wait_recv()
            total = total + rx[r, k - 1].astype(F32)
        gz[r] = total
        gzs[r] = total.astype(BF16)

    loop(R + 1, along_z)
    for k in range(1, Z):
        z_copy(k).start()

    ret_all.wait_recv()
    ret_sib = remote(ret, rets, rsib_sem.at[0], rsib_sem.at[1], sibling)
    ret_sib.start()

    def owner_map(k):
        rows = lax.broadcasted_iota(jnp.int32, (N, HR), 0)
        return jnp.where(sendrow[k] == rows, 1.0, 0.0).astype(BF16)

    added = jnp.transpose(gtT[:, 0:N], (1, 0)) + dot(owner_map(0), ret[...])
    ret_sib.wait_recv()
    gf[...] = (added + dot(owner_map(1), rets[...])).astype(BF16)

    for k in range(1, Z):
        z_copy(k).wait_recv()

    def total_terms(r):
        total = gz[r, z]
        for k in range(1, Z):
            total = total + rz[k - 1, r].astype(F32)
        gw[r] = total

    loop(R + 1, total_terms)

    sib_copy.wait_send()
    halo_all.wait_send()
    ret_all.wait_send()
    ret_sib.wait_send()
    for one in w_copies + w_forwards + ag1 + ag2:
        one.wait_send()

    def sent(r):
        core_copy(r).wait_send()
        for k in range(1, X):
            x_copy(r, k).wait_send()

    loop(R + 1, sent)
    for k in range(1, Z):
        z_copy(k).wait_send()


def shards(X, Z, features, history, weights, cotangent, send_rows, neighbors):
    N, D = features.shape
    R, _, K = neighbors.shape
    O = weights.shape[2]
    Y = lax.axis_size("mp")
    S = D // Y
    CH = X * Z
    SL = CORES * send_rows.shape[2]
    HR = CH * SL
    T = N + HR
    GR = D // (CH * CORES)

    c = lax.rem(lax.axis_index("dom"), CORES)
    chosen = send_rows[0].reshape(CH, CORES, SL // CORES)
    by_core = jnp.stack([jnp.where(c == 0, chosen[:, 0], chosen[:, 1]), jnp.where(c == 0, chosen[:, 1], chosen[:, 0])])
    which = lax.broadcasted_iota(jnp.int32, (2, CH, CORES, SL // CORES), 2)
    slots = jnp.where(which == c, by_core[:, :, None, :], -1).reshape(2, HR)

    dma = pltpu.SemaphoreType.DMA
    vmem = pl.BlockSpec(memory_space=pltpu.VMEM)
    out, gf, gw = pl.pallas_call(
        functools.partial(kernel, X, Z, Y),
        out_shape=(
            jax.ShapeDtypeStruct((N, O), BF16),
            jax.ShapeDtypeStruct((N, S), BF16),
            jax.ShapeDtypeStruct((R + 1, GR, O), F32),
        ),
        in_specs=[vmem, pl.BlockSpec(memory_space=pl.ANY)] + [vmem] * 5,
        out_specs=(vmem, vmem, vmem),
        scratch_shapes=[
            pltpu.VMEM((N, S), F32),
            pltpu.VMEM((2 * N, S), BF16),
            pltpu.VMEM((HR, S), BF16),
            pltpu.VMEM((HR, S), BF16),
            pltpu.VMEM((HR, S), BF16),
            pltpu.VMEM((HR, S), BF16),
            pltpu.VMEM((Y, HR, S), BF16),
            pltpu.VMEM((Y, R + 1, S, O), BF16),
            pltpu.VMEM((R, N, K), jnp.int32),
            pltpu.VMEM((R, N, T), BF16),
            pltpu.VMEM((R, T, O), BF16),
            pltpu.VMEM((R, HR, O), F32),
            pltpu.VMEM((N, O), F32),
            pltpu.VMEM((D, T), BF16),
            pltpu.VMEM((Y, N, O), BF16),
            pltpu.VMEM((O, N), BF16),
            pltpu.VMEM((R, O, T), BF16),
            pltpu.VMEM((R + 1, CH, GR, O), BF16),
            pltpu.VMEM((R + 1, CH, GR, O), F32),
            pltpu.VMEM((R + 1, CH, GR, O), BF16),
            pltpu.VMEM((R + 1, CH, GR, O), BF16),
            pltpu.VMEM((R + 1, X - 1, Z, GR, O), BF16),
            pltpu.VMEM((R + 1, Z, GR, O), F32),
            pltpu.VMEM((R + 1, Z, GR, O), BF16),
            pltpu.VMEM((Z - 1, R + 1, GR, O), BF16),
            pltpu.VMEM((R, S, N), BF16),
            pltpu.VMEM((S, T), F32),
            pltpu.VMEM((HR, S), BF16),
            pltpu.VMEM((HR, S), BF16),
            pltpu.VMEM((HR, S), BF16),
            dma(()),
            dma((2,)),
            dma((2,)),
            dma((2, Y)),
            dma((2, Y)),
            dma((2, 6)),
            dma((2, 6)),
            dma((2, R + 1)),
            dma((2, R + 1, X)),
            dma((2, Z)),
            dma((2,)),
            dma((2,)),
        ],
        compiler_params=pltpu.CompilerParams(
            collective_id=0, has_side_effects=True, vmem_limit_bytes=58 * 1024 * 1024
        ),
        name="graph_layer",
    )(
        features,
        history,
        jnp.transpose(weights, (1, 0, 2)),
        cotangent,
        slots[:, :, None],
        slots[:, None, :],
        jnp.transpose(neighbors, (0, 2, 1)),
    )
    return out, gf, jnp.transpose(gw, (1, 0, 2))


def solution(mesh):
    in_specs = (
        P("dom", None),
        P("dom", None),
        P(None, None, "mp"),
        P("dom", "mp"),
        P("dom", None, None),
        P(None, "dom", None),
    )
    out_specs = (P("dom", "mp"), P("dom", "mp"), P("dom", None, "mp"))
    chips = mesh.shape["dom"] // CORES
    X = 4 if chips >= 8 else 2
    return jax.shard_map(
        functools.partial(shards, X, chips // X), mesh=mesh, in_specs=in_specs, out_specs=out_specs, check_vma=False
    )
```

time: 312 us -> 89.5 us (0.29)
  the two profiles are of different devices: /device:TPU:1 before, /device:TPU:14 now
where the time goes in v1:
time: 89.5 us; the launch traced here: 89.3 us
  Pallas kernels  80.8 us (90%)
  local copies, waits for them, and re-layouts  6.19 us (7%)
  other arithmetic  1.56 us (2%)
    pallas_call x1, Pallas kernels, shards(): pl.pallas_call(functools.partial(kernel, X, Z, Y), out_shape=(jax.ShapeDt...  80.8 us
    unnamed x4, local copies, waits for them, and re-layouts  5.64 us

profile of v1, /device:TPU:14, one launch (start us, length us, event | category | flops | bytes accessed | tf_op | source)
XLA Modules:
  0.0 89.3 jit_solution(7908476448755890318)
XLA Ops:
  0.6 0.1 iota.13
  0.7 0.1 iota.14
  0.8 0.8 copy.25
  1.7 0.1 broadcast_in_dim.25
  1.8 0.6 broadcast_select_fusion.3.sendrow
  2.4 0.2 broadcast_in_dim.24
  2.6 0.9 %broadcast_select_fusion.sendcol = s32[2,512,1]{2,1,0:T(8,128)} fusion(s32[2,512,1]{2,1,0:T(8,128)S(1)} %broadcast_in_dim.24, pred[512]{0:T(512)(128)(4,1)S(1)} %iota.14), kind=kLoop, calls=%fused_computation | loop fusion | flops 1024 | bytes 8704 | tf_op jit(solution)/shard_map/jit(_where)/select_n | solution.py:399
  3.6 80.8 %graph_layer.1 = (bf16[512,256]{1,0:T(8,128)(2,1)}, bf16[512,256]{1,0:T(8,128)(2,1)}, f32[5,16,256]{2,1,0:T(8,128)}) custom-call(bf16[512,1024]{1,0:T(8,128)(2,1)} %feat.1, f32[512,1024]{1,0:T(8,128)} %hist.1, bf16[5,1024,256]{2,1,0:T(8,128)(2,1)} %bitcast.6, bf16[512,256]{1,0:T(8,128)(2,1)} %cot.1, s32[2,512,1]{2,1,0:T(8,128)} %broadcast_select_fusion.sendcol, ...), custom_call_target="tpu_custom_call" | custom-call | tf_op jit(solution)/shard_map/graph_layer/pallas_call | solution.py:403
  84.4 1.7 %copy.34 = bf16[512,256]{1,0:T(8,128)(2,1)} copy(bf16[512,256]{1,0:T(8,128)(2,1)} %get-tuple-element.14) | data formatting | bytes 524288
  86.1 1.7 %copy.35 = bf16[512,256]{1,0:T(8,128)(2,1)} copy(bf16[512,256]{1,0:T(8,128)(2,1)} %get-tuple-element.15) | data formatting | bytes 524288
  87.7 1.5 %copy.36 = f32[16,5,256]{2,0,1:T(8,128)} copy(f32[16,5,256]{2,0,1:T(8,128)} %bitcast.8) | data formatting | bytes 163840
  (4 shorter events, 0.1 us)

commit v2 on v1

--- a/solution.py
+++ b/solution.py
@@ -27,11 +27,11 @@
 
 def kernel(
     X, Z, Y,
-    feat, hist, w, cot, sendcol, sendrow, nbr,
+    feat_in, hist_in, w_in, cot_in, send_in, nbr_in,
     out, gf, gw,
-    histv, src, asib, aown, arecv, slabs, halo, wd, nbrcol, cnt, tab, tacc, pre, tabT,
+    feat, w, cot, nbr, sendT, tcol, sendcol, histv, src, asib, aown, arecv, slabs, halo, wd, nbrcol, cnt, tab, tacc, pre, tabT,
     dp, dT, eT, gsend, gown, grecv, gx, rx, gz, gzs, rz, bT, gtT, hg, ret, rets,
-    hist_sem, sib_sem, halo_sem, w_sem, wf_sem, ag1_sem, ag2_sem, gc_sem, gx_sem, gz_sem, ret_sem, rsib_sem,
+    in_sem, sib_sem, halo_sem, w_sem, wf_sem, ag1_sem, ag2_sem, gc_sem, gx_sem, gz_sem, ret_sem, rsib_sem,
 ):
     N, D = feat.shape
     R = nbr.shape[0]
@@ -43,6 +43,7 @@
     SL = HR // CH
     T = N + HR
     GR = gw.shape[1]
+    SEND = SL // CORES
 
     dom = lax.axis_index("dom")
     y = lax.axis_index("mp")
@@ -65,8 +66,35 @@
     sibling = at(q, 1 - c, y)
     up, down, far = ring(y + 1, Y), ring(y - 1, Y), ring(y + 2, Y)
 
-    hist_copy = pltpu.make_async_copy(hist.at[:, pl.ds(pl.multiple_of(y * S, 128), S)], histv, hist_sem)
-    hist_copy.start()
+    pending = {}
+
+    def wait(name):
+        pending.pop(name)()
+
+    def started(name, copy):
+        copy.start()
+        pending[name] = copy.wait_recv
+        pending[name + " out"] = copy.wait_send
+        return copy
+
+    def finish():
+        for one in list(pending):
+            wait(one)
+
+    columns = pl.ds(pl.multiple_of(y * S, 128), S)
+    inputs = [
+        ("send", send_in, sendT),
+        ("feat slice", feat_in.at[:, columns], src.at[pl.ds(0, N), :]),
+        ("hist", hist_in.at[:, columns], histv),
+        ("nbr", nbr_in, nbr),
+        ("feat", feat_in, feat),
+        ("w", w_in, w),
+        ("cot", cot_in, cot),
+    ]
+    for i, (name, here, there) in enumerate(inputs):
+        cp = pltpu.make_async_copy(here, there, in_sem.at[i])
+        cp.start()
+        pending[name] = cp.wait
 
     barrier = pltpu.get_barrier_semaphore()
 
@@ -78,8 +106,18 @@
         greet(at(q, c, ring(y + k, Y)))
     loop(CH - 1, lambda i: greet(at(lax.rem(q + 1 + i, CH), c, y)))
 
-    src[0:N, :] = feat[:, pl.ds(pl.multiple_of(y * S, 128), S)]
-    hist_copy.wait()
+    wait("send")
+    tcol[...] = jnp.transpose(sendT[...].astype(F32), (1, 0))
+    even, odd = tcol[pl.ds(0, CH, stride=2), :], tcol[pl.ds(1, CH, stride=2), :]
+    slot = lax.broadcasted_iota(jnp.int32, (CH, SL, SEND), 1)
+    lane = lax.broadcasted_iota(jnp.int32, (CH, SL, SEND), 2)
+    taken = slot == lane + c * SEND
+    for k, rows in enumerate((jnp.where(c == 0, even, odd), jnp.where(c == 0, odd, even))):
+        wide = jnp.broadcast_to(rows[:, None, :], (CH, SL, SEND))
+        found = jnp.sum(jnp.where(taken, wide + 1.0, 0.0), axis=2, keepdims=True) - 1.0
+        sendcol[k] = found.reshape(HR, 1).astype(jnp.int32)
+    wait("feat slice")
+    wait("hist")
     src[N : 2 * N, :] = histv[...].astype(BF16)
 
     def pick(k, dst):
@@ -95,10 +133,9 @@
 
     pick(1, asib)
     pl.semaphore_wait(barrier, CH + Y - 1)
-    sib_copy = remote(asib, arecv, sib_sem.at[0], sib_sem.at[1], sibling)
-    sib_copy.start()
+    started("sib", remote(asib, arecv, sib_sem.at[0], sib_sem.at[1], sibling))
     pick(0, aown)
-    sib_copy.wait_recv()
+    wait("sib")
     slabs[...] = aown[...] + arecv[...]
     mine = pl.ds(pl.multiple_of(q * SL, SL), SL)
     halo[y, mine, :] = slabs[mine, :]
@@ -114,9 +151,11 @@
     loop(CH - 1, send_slab)
     others = pl.ds(0, HR - SL)
     halo_all = remote(slabs.at[others, :], halo.at[y, others, :], halo_sem.at[0], halo_sem.at[1], sibling)
+    pending["halo"] = halo_all.wait_recv
+    pending["halo out"] = halo_all.wait_send
 
     half = S // CORES
-    w_copies = []
+    wait("w")
     for k in range(1, Y):
         to = ring(y + k, Y)
         cp = remote(
@@ -124,9 +163,9 @@
             wd.at[y, :, pl.ds(pl.multiple_of(c * half, half), half), :],
             w_sem.at[0, k], w_sem.at[1, k], at(q, c, to),
         )
-        cp.start()
-        w_copies.append(cp)
-
+        started(f"w{k}", cp)
+
+    wait("nbr")
     def counts(r):
         nbrcol[r] = jnp.transpose(nbr[r], (1, 0))
         step = min(32, N)
@@ -147,9 +186,10 @@
     def local_tab(r):
         tab[r, 0:N, :] = dot(feat[...], w[r]).astype(BF16)
 
+    wait("feat")
     loop(R, local_tab)
 
-    def gather_start(buf, sem):
+    def gather_start(name, buf, sem):
         m = buf.shape[1] // 2
         lo, hi = pl.ds(0, m), pl.ds(m, m)
         dev_up, dev_down = at(q, c, up), at(q, c, down)
@@ -161,18 +201,18 @@
             cp(y, lo, 0, dev_up), cp(y, hi, 1, dev_down), cp(y, hi, 2, dev_up), cp(y, lo, 3, dev_down),
             cp(down, lo, 4, dev_up), cp(up, hi, 5, dev_down),
         ]
-        for one in copies[:4]:
-            one.start()
+        for k in range(4):
+            started(f"{name}{k}", copies[k])
         return copies
 
-    def gather_forward(copies):
-        copies[0].wait_recv()
-        copies[4].start()
-        copies[1].wait_recv()
-        copies[5].start()
-
-    halo_all.wait_recv()
-    ag1 = gather_start(halo, ag1_sem)
+    def gather_forward(name, copies):
+        wait(f"{name}0")
+        started(f"{name}4", copies[4])
+        wait(f"{name}1")
+        started(f"{name}5", copies[5])
+
+    wait("halo")
+    ag1 = gather_start("halo", halo, ag1_sem)
 
     pre[...] = dot(feat[...], w[R])
 
@@ -180,7 +220,7 @@
         pre[...] += dot(cnt[r, :, 0:N], tab[r, 0:N, :])
 
     loop(R, local_pre)
-    gather_forward(ag1)
+    gather_forward("halo", ag1)
 
     def add_tab(slot, first):
         rows = pl.ds(pl.multiple_of(slot * S, S), S)
@@ -200,14 +240,14 @@
     add_tab(y, True)
     tabT[:, 0:N] = jnp.transpose(feat[...], (1, 0))
     turn_halo(y)
-    ag1[2].wait_recv()
+    wait("halo2")
     add_tab(down, False)
     turn_halo(down)
-    ag1[3].wait_recv()
+    wait("halo3")
     add_tab(up, False)
     turn_halo(up)
-    ag1[4].wait_recv()
-    ag1[5].wait_recv()
+    wait("halo4")
+    wait("halo5")
     far_rows = pl.ds(pl.multiple_of(far * S, S), S)
 
     def halo_pre(r):
@@ -218,28 +258,26 @@
 
     v = pre[...]
     s = 1.0 / (1.0 + jnp.exp(-v))
+    wait("cot")
     out[...] = (v * s).astype(BF16)
     slope = (cot[...].astype(F32) * (s * (1.0 + v * (1.0 - s)))).astype(BF16)
     dp[y] = slope
-    ag2 = gather_start(dp, ag2_sem)
+    ag2 = gather_start("dp", dp, ag2_sem)
     dT[...] = jnp.transpose(slope, (1, 0))
     turn_halo(far)
 
-    w_forwards = []
     for k in range(1, Y):
         frm = ring(y - k, Y)
-        w_copies[k - 1].wait_recv()
+        wait(f"w{k}")
         part = wd.at[frm, :, pl.ds(pl.multiple_of(c * half, half), half), :]
-        cp = remote(part, part, wf_sem.at[0, k], wf_sem.at[1, k], sibling)
-        cp.start()
-        w_forwards.append(cp)
+        started(f"wf{k}", remote(part, part, wf_sem.at[0, k], wf_sem.at[1, k], sibling))
     wd[y] = w[:, pl.ds(pl.multiple_of(y * S, S), S), :]
 
     def spread_units(r):
         eT[r] = dot(dT[...], cnt[r]).astype(BF16)
 
     loop(R, spread_units)
-    gather_forward(ag2)
+    gather_forward("dp", ag2)
     tile = min(8, CH)
     span = tile * CORES * GR
 
@@ -268,6 +306,8 @@
 
     loop(CH // tile, own_terms)
     core_copy(R).start()
+    pending["core"] = lambda: loop(R + 1, lambda r: core_copy(r).wait_recv())
+    pending["core out"] = lambda: loop(R + 1, lambda r: core_copy(r).wait_send())
 
     def x_copy(r, k):
         to = ring(x + k, X)
@@ -289,11 +329,23 @@
             x_copy(r, k).start()
 
     loop(R + 1, along_x)
+    pending.pop("core")
+
+    def x_wait(r):
+        for k in range(1, X):
+            x_copy(r, k).wait_recv()
+
+    def x_sent(r):
+        for k in range(1, X):
+            x_copy(r, k).wait_send()
+
+    pending["x"] = lambda: loop(R + 1, x_wait)
+    pending["x out"] = lambda: loop(R + 1, x_sent)
 
     for k in (2, 3, 4, 5):
-        ag2[k].wait_recv()
-    for one in w_forwards:
-        one.wait_recv()
+        wait(f"dp{k}")
+    for k in range(1, Y):
+        wait(f"wf{k}")
 
     def back(r):
         total = dot_nt(wd[0, r], dp[0])
@@ -323,6 +375,8 @@
 
     loop(CH - 1, return_slab)
     ret_all = remote(hg.at[others, :], ret.at[others, :], ret_sem.at[0], ret_sem.at[1], sibling)
+    pending["ret"] = ret_all.wait_recv
+    pending["ret out"] = ret_all.wait_send
 
     def z_copy(k):
         to = ring(z + k, Z)
@@ -337,23 +391,24 @@
         gzs[r] = total.astype(BF16)
 
     loop(R + 1, along_z)
+    pending.pop("x")
     for k in range(1, Z):
-        z_copy(k).start()
-
-    ret_all.wait_recv()
-    ret_sib = remote(ret, rets, rsib_sem.at[0], rsib_sem.at[1], sibling)
-    ret_sib.start()
+        started(f"z{k}", z_copy(k))
+
+    wait("ret")
+    started("rets", remote(ret, rets, rsib_sem.at[0], rsib_sem.at[1], sibling))
 
     def owner_map(k):
         rows = lax.broadcasted_iota(jnp.int32, (N, HR), 0)
-        return jnp.where(sendrow[k] == rows, 1.0, 0.0).astype(BF16)
+        named = jnp.transpose(jnp.broadcast_to(sendcol[k], (HR, 8)), (1, 0))[0:1]
+        return jnp.where(named == rows, 1.0, 0.0).astype(BF16)
 
     added = jnp.transpose(gtT[:, 0:N], (1, 0)) + dot(owner_map(0), ret[...])
-    ret_sib.wait_recv()
+    wait("rets")
     gf[...] = (added + dot(owner_map(1), rets[...])).astype(BF16)
 
     for k in range(1, Z):
-        z_copy(k).wait_recv()
+        wait(f"z{k}")
 
     def total_terms(r):
         total = gz[r, z]
@@ -363,21 +418,16 @@
 
     loop(R + 1, total_terms)
 
-    sib_copy.wait_send()
-    halo_all.wait_send()
-    ret_all.wait_send()
-    ret_sib.wait_send()
-    for one in w_copies + w_forwards + ag1 + ag2:
-        one.wait_send()
-
-    def sent(r):
-        core_copy(r).wait_send()
-        for k in range(1, X):
-            x_copy(r, k).wait_send()
-
-    loop(R + 1, sent)
-    for k in range(1, Z):
-        z_copy(k).wait_send()
+    finish()
+
+
+def hand_out(*refs):
+    sem = refs[-1]
+    copies = [pltpu.make_async_copy(refs[i], refs[i + 3], sem.at[i]) for i in range(3)]
+    for one in copies:
+        one.start()
+    for one in copies:
+        one.wait()
 
 
 def shards(X, Z, features, history, weights, cotangent, send_rows, neighbors):
@@ -392,24 +442,26 @@
     T = N + HR
     GR = D // (CH * CORES)
 
-    c = lax.rem(lax.axis_index("dom"), CORES)
-    chosen = send_rows[0].reshape(CH, CORES, SL // CORES)
-    by_core = jnp.stack([jnp.where(c == 0, chosen[:, 0], chosen[:, 1]), jnp.where(c == 0, chosen[:, 1], chosen[:, 0])])
-    which = lax.broadcasted_iota(jnp.int32, (2, CH, CORES, SL // CORES), 2)
-    slots = jnp.where(which == c, by_core[:, :, None, :], -1).reshape(2, HR)
-
     dma = pltpu.SemaphoreType.DMA
     vmem = pl.BlockSpec(memory_space=pltpu.VMEM)
-    out, gf, gw = pl.pallas_call(
+    anywhere = pl.BlockSpec(memory_space=pl.ANY)
+    results = pl.pallas_call(
         functools.partial(kernel, X, Z, Y),
         out_shape=(
             jax.ShapeDtypeStruct((N, O), BF16),
             jax.ShapeDtypeStruct((N, S), BF16),
             jax.ShapeDtypeStruct((R + 1, GR, O), F32),
         ),
-        in_specs=[vmem, pl.BlockSpec(memory_space=pl.ANY)] + [vmem] * 5,
+        in_specs=[anywhere] * 6,
         out_specs=(vmem, vmem, vmem),
         scratch_shapes=[
+            pltpu.VMEM((N, D), BF16),
+            pltpu.VMEM((R + 1, D, O), BF16),
+            pltpu.VMEM((N, O), BF16),
+            pltpu.VMEM((R, K, N), jnp.int32),
+            pltpu.VMEM((SL // CORES, CH * CORES), jnp.int32),
+            pltpu.VMEM((CH * CORES, SL // CORES), F32),
+            pltpu.VMEM((2, HR, 1), jnp.int32),
             pltpu.VMEM((N, S), F32),
             pltpu.VMEM((2 * N, S), BF16),
             pltpu.VMEM((HR, S), BF16),
@@ -440,7 +492,7 @@
             pltpu.VMEM((HR, S), BF16),
             pltpu.VMEM((HR, S), BF16),
             pltpu.VMEM((HR, S), BF16),
-            dma(()),
+            dma((7,)),
             dma((2,)),
             dma((2,)),
             dma((2, Y)),
@@ -462,10 +514,18 @@
         history,
         jnp.transpose(weights, (1, 0, 2)),
         cotangent,
-        slots[:, :, None],
-        slots[:, None, :],
+        jnp.transpose(send_rows[0], (1, 0)),
         jnp.transpose(neighbors, (0, 2, 1)),
     )
+    out, gf, gw = pl.pallas_call(
+        hand_out,
+        out_shape=tuple(jax.ShapeDtypeStruct(one.shape, one.dtype) for one in results),
+        in_specs=[anywhere] * 3,
+        out_specs=(anywhere,) * 3,
+        scratch_shapes=[dma((3,))],
+        compiler_params=pltpu.CompilerParams(vmem_limit_bytes=58 * 1024 * 1024),
+        name="hand_out",
+    )(*results)
     return out, gf, jnp.transpose(gw, (1, 0, 2))
 
 

time: 89.5 us -> 99.4 us (1.11)
  Pallas kernels: 80.8 us -> 98.6 us
  local copies, waits for them, and re-layouts: 6.19 us -> 0 us
  other arithmetic: 1.56 us -> 0 us
    pallas_call x0 -> x1, Pallas kernels: none -> 19.5 us  [shards(): pl.pallas_call(hand_out, out_shape=tuple((jax.ShapeDtypeStruct(one.shape,...]
    unnamed x4 -> x0, local copies, waits for them, and re-layouts: 5.64 us -> none
    pallas_call x1, Pallas kernels: 80.8 us -> 79.1 us  [shards(): pl.pallas_call(functools.partial(kernel, X, Z, Y), out_shape=(jax.ShapeDt...]
    select_n x3 -> x0, other arithmetic: 1.55 us -> none  [the longest x2 1.52 us: shards(): slots = jnp.where(which == c, by_core[:, :, None, :], -1).reshape(2, HR)]
where the time goes in v2:
time: 99.4 us; the launch traced here: 99.3 us
  Pallas kernels  98.6 us (99%)
    pallas_call x1, Pallas kernels, shards(): pl.pallas_call(functools.partial(kernel, X, Z, Y), out_shape=(jax.ShapeDt...  79.1 us
    pallas_call x1, Pallas kernels, shards(): pl.pallas_call(hand_out, out_shape=tuple((jax.ShapeDtypeStruct(one.shape,...  19.5 us

profile of v2, /device:TPU:14, one launch (start us, length us, event | category | flops | bytes accessed | tf_op | source)
XLA Modules:
  0.0 99.3 jit_solution(2837599759062108731)
XLA Ops:
  0.6 79.1 %graph_layer.1 = (bf16[512,256]{1,0:T(8,128)(2,1)}, bf16[512,256]{1,0:T(8,128)(2,1)}, f32[5,16,256]{2,1,0:T(8,128)}) custom-call(bf16[512,1024]{1,0:T(8,128)(2,1)} %feat_in.1, f32[512,1024]{1,0:T(8,128)} %hist_in.1, bf16[5,1024,256]{2,1,0:T(8,128)(2,1)} %bitcast.6, bf16[512,256]{1,0:T(8,128)(2,1)} %cot_in.1, s32[8,64]{1,0:T(8,128)} %bitcast.8, ...), custom_call_target="tpu_custom_call" | custom-call | tf_op jit(solution)/shard_map/graph_layer/pallas_call | solution.py:448
  79.8 19.5 %hand_out.1 = (bf16[512,256]{1,0:T(8,128)(2,1)}, bf16[512,256]{1,0:T(8,128)(2,1)}, f32[5,16,256]{2,1,0:T(8,128)}) custom-call(bf16[512,256]{1,0:T(8,128)(2,1)} %get-tuple-element.9.refs_0_, bf16[512,256]{1,0:T(8,128)(2,1)} %get-tuple-element.10.refs_1_, f32[5,16,256]{2,1,0:T(8,128)} %get-tuple-element.11.refs_2_), custom_call_target="tpu_custom_call" | custom-call | tf_op jit(solution)/shard_map/hand_out/pallas_call | solution.py:520

commit v3 on v2

v3 whole, which is shorter than its diff:
```python
import functools

import jax
import jax.numpy as jnp
from jax import lax
from jax.experimental import pallas as pl
from jax.experimental.pallas import tpu as pltpu
from jax.sharding import PartitionSpec as P

MESH = pl.DeviceIdType.MESH
CORES = 2
HALVES = 2
F32 = jnp.float32
BF16 = jnp.bfloat16


def dot(a, b):
    return jnp.dot(a, b, preferred_element_type=F32)


def dot_nt(a, b):
    return lax.dot_general(a, b, (((1,), (1,)), ((), ())), preferred_element_type=F32)


def loop(count, body):
    lax.fori_loop(0, count, lambda i, c: (body(i), c)[1], 0)


def kernel(
    X, Z, Y,
    feat_in, hist_in, w_in, cot_in, send_in, nbr_in,
    out, gf, gw,
    feat, w, cot, nbr, sendT, tcol, sendcol, histv, src, asib, aown, arecv, slabs, halo, wd, nbrcol, cnt, tab, tacc, pre, tabT,
    dp, dT, eT, bacc, gsend, gown, grecv, gx, rx, gz, gzs, rz, bT, grad, owners, hg, ret, rets,
    in_sem, sib_sem, halo_sem, w_sem, wf_sem, ag1_sem, ag2_sem, gc_sem, gx_sem, gz_sem, ret_sem, rsib_sem,
):
    N, D = feat.shape
    R = nbr.shape[0]
    K = nbr.shape[1]
    O = w.shape[2]
    S = D // Y
    CH = X * Z
    HR = halo.shape[1]
    SL = HR // CH
    T = N + HR
    GR = gw.shape[1]
    SEND = SL // CORES

    dom = lax.axis_index("dom")
    y = lax.axis_index("mp")
    c = lax.rem(dom, CORES)
    q = dom // CORES
    z = lax.rem(q, Z)
    x = q // Z

    def at(chip, core, yy):
        return {"dom": chip * CORES + core, "mp": yy}

    def ring(v, size):
        return lax.rem(v + size, size)

    def remote(s, d, ss, rs, dev):
        return pltpu.make_async_remote_copy(
            src_ref=s, dst_ref=d, send_sem=ss, recv_sem=rs, device_id=dev, device_id_type=MESH
        )

    sibling = at(q, 1 - c, y)
    up, down, far = ring(y + 1, Y), ring(y - 1, Y), ring(y + 2, Y)

    pending = {}

    def wait(name):
        pending.pop(name)()

    def started(name, copy):
        copy.start()
        pending[name] = copy.wait_recv
        pending[name + " out"] = copy.wait_send
        return copy

    def finish():
        for one in list(pending):
            wait(one)

    columns = pl.ds(pl.multiple_of(y * S, 128), S)
    inputs = [
        ("send", send_in, sendT),
        ("feat slice", feat_in.at[:, columns], src.at[pl.ds(0, N), :]),
        ("hist", hist_in.at[:, columns], histv),
        ("nbr", nbr_in, nbr),
        ("feat", feat_in, feat),
        ("w", w_in, w),
        ("cot", cot_in, cot),
    ]
    for i, (name, here, there) in enumerate(inputs):
        cp = pltpu.make_async_copy(here, there, in_sem.at[i])
        cp.start()
        pending[name] = cp.wait

    barrier = pltpu.get_barrier_semaphore()

    def greet(dev):
        pl.semaphore_signal(barrier, inc=1, device_id=dev, device_id_type=MESH)

    greet(sibling)
    for k in range(1, Y):
        greet(at(q, c, ring(y + k, Y)))
    loop(CH - 1, lambda i: greet(at(lax.rem(q + 1 + i, CH), c, y)))

    wait("send")
    tcol[...] = jnp.transpose(sendT[...].astype(F32), (1, 0))
    even, odd = tcol[pl.ds(0, CH, stride=2), :], tcol[pl.ds(1, CH, stride=2), :]
    slot = lax.broadcasted_iota(jnp.int32, (CH, SL, SEND), 1)
    lane = lax.broadcasted_iota(jnp.int32, (CH, SL, SEND), 2)
    taken = slot == lane + c * SEND
    for k, rows in enumerate((jnp.where(c == 0, even, odd), jnp.where(c == 0, odd, even))):
        wide = jnp.broadcast_to(rows[:, None, :], (CH, SL, SEND))
        found = jnp.sum(jnp.where(taken, wide + 1.0, 0.0), axis=2, keepdims=True) - 1.0
        sendcol[k] = found.reshape(HR, 1).astype(jnp.int32)
    wait("feat slice")
    wait("hist")
    src[N : 2 * N, :] = histv[...].astype(BF16)

    def pick(k, dst):
        step = min(128, HR)

        def body(i):
            rows = pl.ds(pl.multiple_of(i * step, step), step)
            col = sendcol[k, rows, :]
            sel = jnp.where(col == lax.broadcasted_iota(jnp.int32, (step, 2 * N), 1), 1.0, 0.0).astype(BF16)
            dst[rows, :] = dot(sel, src[...]).astype(BF16)

        loop(HR // step, body)

    pick(1, asib)
    pl.semaphore_wait(barrier, CH + Y - 1)

    half = S // CORES
    half_rows = pl.ds(pl.multiple_of(c * half, half), half)

    def send_weights(k):
        to = ring(y + k, Y)
        rows = pl.ds(pl.multiple_of(to * S + c * half, half), half)
        part = w.at[:, rows, :]
        started(f"w{k}", remote(part, wd.at[y, :, half_rows, :], w_sem.at[0, k], w_sem.at[1, k], at(q, c, to)))

    def forward_weights(k):
        wait(f"w{k}")
        part = wd.at[ring(y - k, Y), :, half_rows, :]
        started(f"wf{k}", remote(part, part, wf_sem.at[0, k], wf_sem.at[1, k], sibling))

    wait("w")
    send_weights(1)
    send_weights(3)
    started("sib", remote(asib, arecv, sib_sem.at[0], sib_sem.at[1], sibling))
    pick(0, aown)
    wait("sib")
    slabs[...] = aown[...] + arecv[...]
    mine = pl.ds(pl.multiple_of(q * SL, SL), SL)
    halo[y, mine, :] = slabs[mine, :]

    def chip_rows(i):
        chip = lax.rem(q + 1 + i, CH)
        return chip, pl.ds(pl.multiple_of(chip * SL, SL), SL)

    others = pl.ds(0, HR - SL)
    part_cols = [pl.ds(h * (S // HALVES), S // HALVES) for h in range(HALVES)]
    for h, cols in enumerate(part_cols):
        sems = halo_sem.at[0, h], halo_sem.at[1, h]

        def send_slab(i):
            chip, rows = chip_rows(i)
            remote(slabs.at[rows, cols], halo.at[y, mine, cols], *sems, at(chip, c, y)).start()

        loop(CH - 1, send_slab)
        everything = remote(slabs.at[others, cols], halo.at[y, others, cols], *sems, sibling)
        pending[f"slabs{h}"] = everything.wait_recv
        pending[f"slabs{h} out"] = everything.wait_send

    wait("nbr")

    def counts(r):
        nbrcol[r] = jnp.transpose(nbr[r], (1, 0))
        step = min(32, N)

        def body(i):
            rows = pl.ds(pl.multiple_of(i * step, step), step)
            cols = nbrcol[r, rows, :]
            pos = lax.broadcasted_iota(jnp.int32, (step, T), 1)
            total = jnp.zeros((step, T), F32)
            for k in range(K):
                total = total + jnp.where(cols[:, k : k + 1] == pos, 1.0 / K, 0.0)
            cnt[r, rows, :] = total.astype(BF16)

        loop(N // step, body)

    def gather_start(name, buf, cols, sem):
        m = buf.shape[1] // 2
        lo, hi = pl.ds(0, m), pl.ds(m, m)
        dev_up, dev_down = at(q, c, up), at(q, c, down)

        def cp(slot, rows, k, dev):
            part = buf.at[slot, rows, cols]
            return remote(part, part, sem.at[0, k], sem.at[1, k], dev)

        copies = [
            cp(y, lo, 0, dev_up), cp(y, hi, 1, dev_down), cp(y, hi, 2, dev_up), cp(y, lo, 3, dev_down),
            cp(down, lo, 4, dev_up), cp(up, hi, 5, dev_down),
        ]
        for k in range(4):
            started(f"{name}{k}", copies[k])
        return copies

    def gather_forward(name, copies):
        wait(f"{name}0")
        started(f"{name}4", copies[4])
        wait(f"{name}1")
        started(f"{name}5", copies[5])

    def wait_halo(k):
        for h in range(HALVES):
            wait(f"halo{h}{k}")

    def local_tab(r):
        tab[r, 0:N, :] = dot(feat[...], w[r]).astype(BF16)

    def slot_rows(slot):
        return pl.ds(pl.multiple_of(slot * S, S), S)

    def turn_halo(slot):
        tabT[slot_rows(slot), N:T] = jnp.transpose(halo[slot], (1, 0))

    gathers = {}

    def gather_halo(h):
        wait(f"slabs{h}")
        gathers[h] = gather_start(f"halo{h}", halo, part_cols[h], ag1_sem.at[h])

    loop(R // 2, counts)
    gather_halo(0)
    wait("feat")
    loop(R, local_tab)
    gather_halo(1)
    gather_forward("halo0", gathers[0])
    loop(R - R // 2, lambda r: counts(r + R // 2))
    gather_forward("halo1", gathers[1])

    local = dot(feat[...], w[R])
    for r in range(R):
        local = local + dot(cnt[r, :, 0:N], tab[r, 0:N, :])
    pre[...] = local

    def own_tab(r):
        tacc[r] = dot(halo[y], w[r, slot_rows(y), :])

    def near_tab(r):
        tacc[r] += dot(halo[down], w[r, slot_rows(down), :]) + dot(halo[up], w[r, slot_rows(up), :])

    loop(R, own_tab)
    tabT[:, 0:N] = jnp.transpose(feat[...], (1, 0))
    turn_halo(y)
    wait_halo(2)
    wait_halo(3)
    loop(R, near_tab)
    turn_halo(down)
    turn_halo(up)
    wait_halo(4)
    wait_halo(5)
    send_weights(2)

    def far_tab(r):
        tab[r, N:T, :] = (tacc[r] + dot(halo[far], w[r, slot_rows(far), :])).astype(BF16)

    loop(R, far_tab)
    total = pre[...]
    for r in range(R):
        total = total + dot(cnt[r, :, N:T], tab[r, N:T, :])
    pre[...] = total

    wait("cot")
    tile = min(64, N)

    def activate(i):
        rows = pl.ds(pl.multiple_of(i * tile, tile), tile)
        v = pre[rows, :]
        s = 1.0 / (1.0 + jnp.exp(-v))
        out[rows, :] = (v * s).astype(BF16)
        dp[y, rows, :] = (cot[rows, :].astype(F32) * (s * (1.0 + v * (1.0 - s)))).astype(BF16)

    loop(N // tile, activate)
    ag2 = gather_start("dp", dp, pl.ds(0, O), ag2_sem)
    dT[...] = jnp.transpose(dp[y], (1, 0))
    turn_halo(far)

    def core_copy(p):
        return remote(gsend.at[p], grecv.at[p], gc_sem.at[0, p], gc_sem.at[1, p], sibling)

    def put_terms(p, part):
        part = part.reshape(CH, CORES, GR, O)
        gown[p] = jnp.where(c == 0, part[:, 0], part[:, 1])
        gsend[p] = jnp.where(c == 0, part[:, 1], part[:, 0]).astype(BF16)
        started(f"core{p}", core_copy(p))

    def relation_terms(r):
        eT[r] = dot(dT[...], cnt[r]).astype(BF16)
        put_terms(r + 1, dot_nt(tabT[...], eT[r]))

    def x_copy(p, k):
        to = ring(x + k, X)
        return remote(
            gx.at[p, pl.ds(to * Z, Z)], rx.at[p, k - 1], gx_sem.at[0, p, k], gx_sem.at[1, p, k], at(to * Z + z, c, y)
        )

    def along_x(p):
        wait(f"core{p}")
        some = min(8, CH)

        def body(i):
            chips = pl.ds(i * some, some)
            total = gown[p, chips] + grecv[p, chips].astype(F32)
            gown[p, chips] = total
            gx[p, chips] = total.astype(BF16)

        loop(CH // some, body)
        for k in range(1, X):
            started(f"x{p}{k}", x_copy(p, k))

    put_terms(0, dot(tabT[:, 0:N], dp[y]))
    relation_terms(0)
    along_x(0)
    gather_forward("dp", ag2)
    for r in range(1, R):
        relation_terms(r)
        along_x(r)
    forward_weights(1)
    forward_weights(3)
    along_x(R)
    forward_weights(2)

    def own_back(r):
        bacc[r] = dot_nt(w[r, slot_rows(y), :], dp[y])

    def near_back(r):
        bacc[r] += dot_nt(wd[down, r], dp[down]) + dot_nt(wd[up, r], dp[up])

    def far_back(r):
        bT[r] = (bacc[r] + dot_nt(wd[far, r], dp[far])).astype(BF16)

    loop(R + 1, own_back)
    for k in (1, 3):
        wait(f"wf{k}")
    for k in (2, 3):
        wait(f"dp{k}")
    loop(R + 1, near_back)
    wait("wf2")
    for k in (4, 5):
        wait(f"dp{k}")
    loop(R, far_back)
    received = dot(bT[0], cnt[0, :, N:T])
    for r in range(1, R):
        received = received + dot(bT[r], cnt[r, :, N:T])

    hg[...] = jnp.transpose(received, (1, 0)).astype(BF16)
    ret[mine, :] = hg[mine, :]

    def return_slab(i):
        chip, rows = chip_rows(i)
        remote(hg.at[rows, :], ret.at[mine, :], ret_sem.at[0], ret_sem.at[1], at(chip, c, y)).start()

    loop(CH - 1, return_slab)
    ret_all = remote(hg.at[others, :], ret.at[others, :], ret_sem.at[0], ret_sem.at[1], sibling)
    pending["ret"] = ret_all.wait_recv
    pending["ret out"] = ret_all.wait_send

    own = bacc[R] + dot_nt(wd[far, R], dp[far])
    for r in range(R):
        own = own + dot(bT[r], cnt[r, :, 0:N])
    grad[...] = jnp.transpose(own, (1, 0))

    def z_copy(g, places, k):
        to = ring(z + k, Z)
        return remote(
            gzs.at[places, to], rz.at[k - 1, places], gz_sem.at[0, g, k], gz_sem.at[1, g, k], at(x * Z + to, c, y)
        )

    def along_z(g, first, last):
        for p in range(first, last):
            total = gown[p, pl.ds(x * Z, Z)]
            for k in range(1, X):
                wait(f"x{p}{k}")
                total = total + rx[p, k - 1].astype(F32)
            gz[p] = total
            gzs[p] = total.astype(BF16)
        for k in range(1, Z):
            started(f"z{g}{k}", z_copy(g, pl.ds(first, last - first), k))

    first_group = (R + 2) // 2
    along_z(0, 0, first_group)

    def owner_map(k):
        rows = lax.broadcasted_iota(jnp.int32, (N, HR), 0)
        named = jnp.transpose(jnp.broadcast_to(sendcol[k], (HR, 8)), (1, 0))[0:1]
        return jnp.where(named == rows, 1.0, 0.0).astype(BF16)

    for k in range(2):
        owners[k] = owner_map(k)
    along_z(1, first_group, R + 1)

    wait("ret")
    started("rets", remote(ret, rets, rsib_sem.at[0], rsib_sem.at[1], sibling))
    grad[...] += dot(owners[0], ret[...])
    wait("rets")
    gf[...] = (grad[...] + dot(owners[1], rets[...])).astype(BF16)

    def total_terms(p, r):
        total = gz[p, z]
        for k in range(1, Z):
            total = total + rz[k - 1, p].astype(F32)
        gw[r] = total

    for k in range(1, Z):
        wait(f"z0{k}")
        wait(f"z1{k}")
    total_terms(0, R)
    loop(R, lambda r: total_terms(r + 1, r))
    finish()


def hand_out(*refs):
    for here, there in zip(refs[:3], refs[3:]):
        there[...] = here[...]


def shards(X, Z, features, history, weights, cotangent, send_rows, neighbors):
    N, D = features.shape
    R, _, K = neighbors.shape
    O = weights.shape[2]
    Y = lax.axis_size("mp")
    S = D // Y
    CH = X * Z
    SL = CORES * send_rows.shape[2]
    HR = CH * SL
    T = N + HR
    GR = D // (CH * CORES)

    dma = pltpu.SemaphoreType.DMA
    vmem = pl.BlockSpec(memory_space=pltpu.VMEM)
    anywhere = pl.BlockSpec(memory_space=pl.ANY)
    results = pl.pallas_call(
        functools.partial(kernel, X, Z, Y),
        out_shape=(
            jax.ShapeDtypeStruct((N, O), BF16),
            jax.ShapeDtypeStruct((N, S), BF16),
            jax.ShapeDtypeStruct((R + 1, GR, O), F32),
        ),
        in_specs=[anywhere] * 6,
        out_specs=(vmem, vmem, vmem),
        scratch_shapes=[
            pltpu.VMEM((N, D), BF16),
            pltpu.VMEM((R + 1, D, O), BF16),
            pltpu.VMEM((N, O), BF16),
            pltpu.VMEM((R, K, N), jnp.int32),
            pltpu.VMEM((SL // CORES, CH * CORES), jnp.int32),
            pltpu.VMEM((CH * CORES, SL // CORES), F32),
            pltpu.VMEM((2, HR, 1), jnp.int32),
            pltpu.VMEM((N, S), F32),
            pltpu.VMEM((2 * N, S), BF16),
            pltpu.VMEM((HR, S), BF16),
            pltpu.VMEM((HR, S), BF16),
            pltpu.VMEM((HR, S), BF16),
            pltpu.VMEM((HR, S), BF16),
            pltpu.VMEM((Y, HR, S), BF16),
            pltpu.VMEM((Y, R + 1, S, O), BF16),
            pltpu.VMEM((R, N, K), jnp.int32),
            pltpu.VMEM((R, N, T), BF16),
            pltpu.VMEM((R, T, O), BF16),
            pltpu.VMEM((R, HR, O), F32),
            pltpu.VMEM((N, O), F32),
            pltpu.VMEM((D, T), BF16),
            pltpu.VMEM((Y, N, O), BF16),
            pltpu.VMEM((O, N), BF16),
            pltpu.VMEM((R, O, T), BF16),
            pltpu.VMEM((R + 1, S, N), F32),
            pltpu.VMEM((R + 1, CH, GR, O), BF16),
            pltpu.VMEM((R + 1, CH, GR, O), F32),
            pltpu.VMEM((R + 1, CH, GR, O), BF16),
            pltpu.VMEM((R + 1, CH, GR, O), BF16),
            pltpu.VMEM((R + 1, X - 1, Z, GR, O), BF16),
            pltpu.VMEM((R + 1, Z, GR, O), F32),
            pltpu.VMEM((R + 1, Z, GR, O), BF16),
            pltpu.VMEM((Z - 1, R + 1, GR, O), BF16),
            pltpu.VMEM((R, S, N), BF16),
            pltpu.VMEM((N, S), F32),
            pltpu.VMEM((2, N, HR), BF16),
            pltpu.VMEM((HR, S), BF16),
            pltpu.VMEM((HR, S), BF16),
            pltpu.VMEM((HR, S), BF16),
            dma((7,)),
            dma((2,)),
            dma((2, HALVES)),
            dma((2, Y)),
            dma((2, Y)),
            dma((HALVES, 2, 6)),
            dma((2, 6)),
            dma((2, R + 1)),
            dma((2, R + 1, X)),
            dma((2, 2, Z)),
            dma((2,)),
            dma((2,)),
        ],
        compiler_params=pltpu.CompilerParams(
            collective_id=0, has_side_effects=True, vmem_limit_bytes=58 * 1024 * 1024
        ),
        name="graph_layer",
    )(
        features,
        history,
        jnp.transpose(weights, (1, 0, 2)),
        cotangent,
        jnp.transpose(send_rows[0], (1, 0)),
        jnp.transpose(neighbors, (0, 2, 1)),
    )
    out, gf, gw = pl.pallas_call(
        hand_out,
        out_shape=tuple(jax.ShapeDtypeStruct(one.shape, one.dtype) for one in results),
        in_specs=[vmem] * 3,
        out_specs=(vmem,) * 3,
        name="hand_out",
    )(*results)
    return out, gf, jnp.transpose(gw, (1, 0, 2))


def solution(mesh):
    in_specs = (
        P("dom", None),
        P("dom", None),
        P(None, None, "mp"),
        P("dom", "mp"),
        P("dom", None, None),
        P(None, "dom", None),
    )
    out_specs = (P("dom", "mp"), P("dom", "mp"), P("dom", None, "mp"))
    chips = mesh.shape["dom"] // CORES
    X = 4 if chips >= 8 else 2
    return jax.shard_map(
        functools.partial(shards, X, chips // X), mesh=mesh, in_specs=in_specs, out_specs=out_specs, check_vma=False
    )
```

time: 99.4 us -> 79.2 us (0.80)
  the two profiles are of different devices: /device:TPU:14 before, /device:TPU:1 now
where the time goes in v3:
time: 79.2 us; the launch traced here: 79.1 us
  Pallas kernels  78.5 us (99%)
    pallas_call x1, Pallas kernels, shards(): pl.pallas_call(functools.partial(kernel, X, Z, Y), out_shape=(jax.ShapeDt...  76.6 us
    pallas_call x1, Pallas kernels, shards(): pl.pallas_call(hand_out, out_shape=tuple((jax.ShapeDtypeStruct(one.shape,...  1.87 us

profile of v3, /device:TPU:1, one launch (start us, length us, event | category | flops | bytes accessed | tf_op | source)
XLA Modules:
  0.0 79.1 jit_solution(18159256801918349500)
XLA Ops:
  0.6 76.6 %graph_layer.1 = (bf16[512,256]{1,0:T(8,128)(2,1)}, bf16[512,256]{1,0:T(8,128)(2,1)}, f32[5,16,256]{2,1,0:T(8,128)}) custom-call(bf16[512,1024]{1,0:T(8,128)(2,1)} %feat_in.1, f32[512,1024]{1,0:T(8,128)} %hist_in.1, bf16[5,1024,256]{2,1,0:T(8,128)(2,1)} %bitcast.6, bf16[512,256]{1,0:T(8,128)(2,1)} %cot_in.1, s32[8,64]{1,0:T(8,128)} %bitcast.8, ...), custom_call_target="tpu_custom_call" | custom-call | tf_op jit(solution)/shard_map/graph_layer/pallas_call | solution.py:449
  77.3 1.9 %hand_out.1 = (bf16[512,256]{1,0:T(8,128)(2,1)}, bf16[512,256]{1,0:T(8,128)(2,1)}, f32[5,16,256]{2,1,0:T(8,128)}) custom-call(bf16[512,256]{1,0:T(8,128)(2,1)} %get-tuple-element.9.refs_0_, bf16[512,256]{1,0:T(8,128)(2,1)} %get-tuple-element.10.refs_1_, f32[5,16,256]{2,1,0:T(8,128)} %get-tuple-element.11.refs_2_), custom_call_target="tpu_custom_call" | custom-call | tf_op jit(solution)/shard_map/hand_out/pallas_call | solution.py:523

commit v4 on v3

--- a/solution.py
+++ b/solution.py
@@ -31,8 +31,8 @@
     feat_in, hist_in, w_in, cot_in, send_in, nbr_in,
     out, gf, gw,
     feat, w, cot, nbr, sendT, tcol, sendcol, histv, src, asib, aown, arecv, slabs, halo, wd, nbrcol, cnt, tab, tacc, pre, tabT,
-    dp, dT, eT, bacc, gsend, gown, grecv, gx, rx, gz, gzs, rz, bT, grad, owners, hg, ret, rets,
-    in_sem, sib_sem, halo_sem, w_sem, wf_sem, ag1_sem, ag2_sem, gc_sem, gx_sem, gz_sem, ret_sem, rsib_sem,
+    dp, dT, eT, bacc, gsend, gown, grecv, gx, relay, rx, gz, gzs, rz, bT, grad, owners, hg, ret, rets,
+    in_sem, sib_sem, halo_sem, w_sem, wf_sem, ag1_sem, ag2_sem, gc_sem, gr_sem, gx_sem, gz_sem, ret_sem, rsib_sem,
 ):
     N, D = feat.shape
     R = nbr.shape[0]
@@ -122,15 +122,16 @@
     src[N : 2 * N, :] = histv[...].astype(BF16)
 
     def pick(k, dst):
-        step = min(128, HR)
+        step = min(256, HR)
 
         def body(i):
-            rows = pl.ds(pl.multiple_of(i * step, step), step)
+            rows = pl.ds(i * step, step)
             col = sendcol[k, rows, :]
             sel = jnp.where(col == lax.broadcasted_iota(jnp.int32, (step, 2 * N), 1), 1.0, 0.0).astype(BF16)
             dst[rows, :] = dot(sel, src[...]).astype(BF16)
 
-        loop(HR // step, body)
+        for i in range(HR // step):
+            body(i)
 
     pick(1, asib)
     pl.semaphore_wait(barrier, CH + Y - 1)
@@ -152,6 +153,7 @@
     wait("w")
     send_weights(1)
     send_weights(3)
+    send_weights(2)
     started("sib", remote(asib, arecv, sib_sem.at[0], sib_sem.at[1], sibling))
     pick(0, aown)
     wait("sib")
@@ -181,16 +183,17 @@
 
     def counts(r):
         nbrcol[r] = jnp.transpose(nbr[r], (1, 0))
-        step = min(32, N)
+        step = min(128, N)
+        share, none = jnp.asarray(1.0 / K, BF16), jnp.asarray(0.0, BF16)
 
         def body(i):
             rows = pl.ds(pl.multiple_of(i * step, step), step)
-            cols = nbrcol[r, rows, :]
-            pos = lax.broadcasted_iota(jnp.int32, (step, T), 1)
-            total = jnp.zeros((step, T), F32)
+            cols = nbrcol[r, rows, :].astype(jnp.int16)
+            pos = lax.broadcasted_iota(jnp.int16, (step, T), 1)
+            total = jnp.zeros((step, T), BF16)
             for k in range(K):
-                total = total + jnp.where(cols[:, k : k + 1] == pos, 1.0 / K, 0.0)
-            cnt[r, rows, :] = total.astype(BF16)
+                total = total + jnp.where(jnp.broadcast_to(cols[:, k : k + 1], (step, T)) == pos, share, none)
+            cnt[r, rows, :] = total
 
         loop(N // step, body)
 
@@ -236,19 +239,18 @@
         wait(f"slabs{h}")
         gathers[h] = gather_start(f"halo{h}", halo, part_cols[h], ag1_sem.at[h])
 
-    loop(R // 2, counts)
+    loop(R, counts)
+    wait("feat")
     gather_halo(0)
-    wait("feat")
     loop(R, local_tab)
     gather_halo(1)
     gather_forward("halo0", gathers[0])
-    loop(R - R // 2, lambda r: counts(r + R // 2))
-    gather_forward("halo1", gathers[1])
 
     local = dot(feat[...], w[R])
     for r in range(R):
         local = local + dot(cnt[r, :, 0:N], tab[r, 0:N, :])
     pre[...] = local
+    gather_forward("halo1", gathers[1])
 
     def own_tab(r):
         tacc[r] = dot(halo[y], w[r, slot_rows(y), :])
@@ -266,19 +268,19 @@
     turn_halo(up)
     wait_halo(4)
     wait_halo(5)
-    send_weights(2)
 
     def far_tab(r):
         tab[r, N:T, :] = (tacc[r] + dot(halo[far], w[r, slot_rows(far), :])).astype(BF16)
 
-    loop(R, far_tab)
+    for r in range(R):
+        far_tab(r)
     total = pre[...]
     for r in range(R):
         total = total + dot(cnt[r, :, N:T], tab[r, N:T, :])
     pre[...] = total
 
     wait("cot")
-    tile = min(64, N)
+    tile = min(128, N)
 
     def activate(i):
         rows = pl.ds(pl.multiple_of(i * tile, tile), tile)
@@ -305,13 +307,13 @@
         eT[r] = dot(dT[...], cnt[r]).astype(BF16)
         put_terms(r + 1, dot_nt(tabT[...], eT[r]))
 
-    def x_copy(p, k):
-        to = ring(x + k, X)
-        return remote(
-            gx.at[p, pl.ds(to * Z, Z)], rx.at[p, k - 1], gx_sem.at[0, p, k], gx_sem.at[1, p, k], at(to * Z + z, c, y)
-        )
-
-    def along_x(p):
+    x_up, x_down, x_far = ring(x + 1, X), ring(x - 1, X), ring(x + 2, X)
+    zh = Z // 2
+
+    def x_copy(p, k, block, to):
+        return remote(block, rx.at[p, k], gx_sem.at[0, p, k], gx_sem.at[1, p, k], at(to * Z + z, c, y))
+
+    def far_x(p):
         wait(f"core{p}")
         some = min(8, CH)
 
@@ -322,19 +324,33 @@
             gx[p, chips] = total.astype(BF16)
 
         loop(CH // some, body)
-        for k in range(1, X):
-            started(f"x{p}{k}", x_copy(p, k))
+        for k, to in enumerate((x_up, x_down)):
+            block = gx.at[p, pl.ds(x_far * Z + k * zh, zh)]
+            sems = gr_sem.at[0, p, k], gr_sem.at[1, p, k]
+            started(f"r{p}{k}", remote(block, relay.at[p, k], *sems, at(to * Z + z, c, y)))
+
+    def near_x(p):
+        for k, to in enumerate((x_up, x_down)):
+            wait(f"r{p}{k}")
+            part = pl.ds(to * Z + k * zh, zh)
+            gx[p, part] = (gown[p, part] + relay[p, k].astype(F32)).astype(BF16)
+            started(f"x{p}{k}", x_copy(p, k, gx.at[p, pl.ds(to * Z, Z)], to))
 
     put_terms(0, dot(tabT[:, 0:N], dp[y]))
     relation_terms(0)
-    along_x(0)
+    far_x(0)
+    relation_terms(1)
+    far_x(1)
     gather_forward("dp", ag2)
-    for r in range(1, R):
+    near_x(0)
+    for r in range(2, R):
         relation_terms(r)
-        along_x(r)
+        far_x(r)
+        near_x(r - 1)
+    far_x(R)
     forward_weights(1)
     forward_weights(3)
-    along_x(R)
+    near_x(R - 1)
     forward_weights(2)
 
     def own_back(r):
@@ -347,6 +363,7 @@
         bT[r] = (bacc[r] + dot_nt(wd[far, r], dp[far])).astype(BF16)
 
     loop(R + 1, own_back)
+    near_x(R)
     for k in (1, 3):
         wait(f"wf{k}")
     for k in (2, 3):
@@ -355,7 +372,8 @@
     wait("wf2")
     for k in (4, 5):
         wait(f"dp{k}")
-    loop(R, far_back)
+    for r in range(R):
+        far_back(r)
     received = dot(bT[0], cnt[0, :, N:T])
     for r in range(1, R):
         received = received + dot(bT[r], cnt[r, :, N:T])
@@ -386,9 +404,9 @@
     def along_z(g, first, last):
         for p in range(first, last):
             total = gown[p, pl.ds(x * Z, Z)]
-            for k in range(1, X):
+            for k in range(2):
                 wait(f"x{p}{k}")
-                total = total + rx[p, k - 1].astype(F32)
+                total = total + rx[p, k].astype(F32)
             gz[p] = total
             gzs[p] = total.astype(BF16)
         for k in range(1, Z):
@@ -485,7 +503,8 @@
             pltpu.VMEM((R + 1, CH, GR, O), F32),
             pltpu.VMEM((R + 1, CH, GR, O), BF16),
             pltpu.VMEM((R + 1, CH, GR, O), BF16),
-            pltpu.VMEM((R + 1, X - 1, Z, GR, O), BF16),
+            pltpu.VMEM((R + 1, 2, Z // 2, GR, O), BF16),
+            pltpu.VMEM((R + 1, 2, Z, GR, O), BF16),
             pltpu.VMEM((R + 1, Z, GR, O), F32),
             pltpu.VMEM((R + 1, Z, GR, O), BF16),
             pltpu.VMEM((Z - 1, R + 1, GR, O), BF16),
@@ -503,7 +522,8 @@
             dma((HALVES, 2, 6)),
             dma((2, 6)),
             dma((2, R + 1)),
-            dma((2, R + 1, X)),
+            dma((2, R + 1, 2)),
+            dma((2, R + 1, 2)),
             dma((2, 2, Z)),
             dma((2,)),
             dma((2,)),

time: 79.2 us -> 73.4 us (0.927)
  Pallas kernels: 78.5 us -> 72.6 us
    pallas_call x1, Pallas kernels: 76.6 us -> 70.7 us  [shards(): pl.pallas_call(functools.partial(kernel, X, Z, Y), out_shape=(jax.ShapeDt...]
where the time goes in v4:
time: 73.4 us; the launch traced here: 73.2 us
  Pallas kernels  72.6 us (99%)
    pallas_call x1, Pallas kernels, shards(): pl.pallas_call(functools.partial(kernel, X, Z, Y), out_shape=(jax.ShapeDt...  70.7 us
    pallas_call x1, Pallas kernels, shards(): pl.pallas_call(hand_out, out_shape=tuple((jax.ShapeDtypeStruct(one.shape,...  1.87 us

profile of v4, /device:TPU:1, one launch (start us, length us, event | category | flops | bytes accessed | tf_op | source)
XLA Modules:
  0.0 73.2 jit_solution(928852322385717876)
XLA Ops:
  0.6 70.7 %graph_layer.1 = (bf16[512,256]{1,0:T(8,128)(2,1)}, bf16[512,256]{1,0:T(8,128)(2,1)}, f32[5,16,256]{2,1,0:T(8,128)}) custom-call(bf16[512,1024]{1,0:T(8,128)(2,1)} %feat_in.1, f32[512,1024]{1,0:T(8,128)} %hist_in.1, bf16[5,1024,256]{2,1,0:T(8,128)(2,1)} %bitcast.6, bf16[512,256]{1,0:T(8,128)(2,1)} %cot_in.1, s32[8,64]{1,0:T(8,128)} %bitcast.8, ...), custom_call_target="tpu_custom_call" | custom-call | tf_op jit(solution)/shard_map/graph_layer/pallas_call | solution.py:467
  71.3 1.9 %hand_out.1 = (bf16[512,256]{1,0:T(8,128)(2,1)}, bf16[512,256]{1,0:T(8,128)(2,1)}, f32[5,16,256]{2,1,0:T(8,128)}) custom-call(bf16[512,256]{1,0:T(8,128)(2,1)} %get-tuple-element.9.refs_0_, bf16[512,256]{1,0:T(8,128)(2,1)} %get-tuple-element.10.refs_1_, f32[5,16,256]{2,1,0:T(8,128)} %get-tuple-element.11.refs_2_), custom_call_target="tpu_custom_call" | custom-call | tf_op jit(solution)/shard_map/hand_out/pallas_call | solution.py:543

commit v5 on v4

--- a/solution.py
+++ b/solution.py
@@ -32,7 +32,7 @@
     out, gf, gw,
     feat, w, cot, nbr, sendT, tcol, sendcol, histv, src, asib, aown, arecv, slabs, halo, wd, nbrcol, cnt, tab, tacc, pre, tabT,
     dp, dT, eT, bacc, gsend, gown, grecv, gx, relay, rx, gz, gzs, rz, bT, grad, owners, hg, ret, rets,
-    in_sem, sib_sem, halo_sem, w_sem, wf_sem, ag1_sem, ag2_sem, gc_sem, gr_sem, gx_sem, gz_sem, ret_sem, rsib_sem,
+    in_sem, sib_sem, halo_sem, w_sem, wx_sem, wf_sem, ag1_sem, ag2_sem, gc_sem, gr_sem, gx_sem, gz_sem, ret_sem, rsib_sem,
 ):
     N, D = feat.shape
     R = nbr.shape[0]
@@ -126,8 +126,9 @@
 
         def body(i):
             rows = pl.ds(i * step, step)
-            col = sendcol[k, rows, :]
-            sel = jnp.where(col == lax.broadcasted_iota(jnp.int32, (step, 2 * N), 1), 1.0, 0.0).astype(BF16)
+            col = jnp.broadcast_to(sendcol[k, rows, :].astype(jnp.int16), (step, 2 * N))
+            named = col == lax.broadcasted_iota(jnp.int16, (step, 2 * N), 1)
+            sel = jnp.where(named, jnp.asarray(1.0, BF16), jnp.asarray(0.0, BF16))
             dst[rows, :] = dot(sel, src[...]).astype(BF16)
 
         for i in range(HR // step):
@@ -137,18 +138,29 @@
     pl.semaphore_wait(barrier, CH + Y - 1)
 
     half = S // CORES
+    piece = half // X
     half_rows = pl.ds(pl.multiple_of(c * half, half), half)
+    piece_rows = pl.ds(pl.multiple_of(c * half + x * piece, piece), piece)
 
     def send_weights(k):
         to = ring(y + k, Y)
-        rows = pl.ds(pl.multiple_of(to * S + c * half, half), half)
-        part = w.at[:, rows, :]
-        started(f"w{k}", remote(part, wd.at[y, :, half_rows, :], w_sem.at[0, k], w_sem.at[1, k], at(q, c, to)))
-
-    def forward_weights(k):
-        wait(f"w{k}")
-        part = wd.at[ring(y - k, Y), :, half_rows, :]
-        started(f"wf{k}", remote(part, part, wf_sem.at[0, k], wf_sem.at[1, k], sibling))
+        rows = pl.ds(pl.multiple_of(to * S + c * half + x * piece, piece), piece)
+        sems = w_sem.at[0, k], w_sem.at[1, k]
+        started(f"w{k}", remote(w.at[:, rows, :], wd.at[k - 1, :, piece_rows, :], *sems, at(q, c, to)))
+
+    def share_weights():
+        for k in range(1, Y):
+            wait(f"w{k}")
+        part = wd.at[:, :, piece_rows, :]
+        for k in range(1, X):
+            to = at(ring(x + k, X) * Z + z, c, y)
+            started(f"wx{k}", remote(part, part, wx_sem.at[0, k], wx_sem.at[1, k], to))
+
+    def pass_weights():
+        for k in range(1, X):
+            wait(f"wx{k}")
+        part = wd.at[:, :, half_rows, :]
+        started("wf", remote(part, part, wf_sem.at[0], wf_sem.at[1], sibling))
 
     wait("w")
     send_weights(1)
@@ -245,6 +257,7 @@
     loop(R, local_tab)
     gather_halo(1)
     gather_forward("halo0", gathers[0])
+    share_weights()
 
     local = dot(feat[...], w[R])
     for r in range(R):
@@ -290,7 +303,21 @@
         dp[y, rows, :] = (cot[rows, :].astype(F32) * (s * (1.0 + v * (1.0 - s)))).astype(BF16)
 
     loop(N // tile, activate)
-    ag2 = gather_start("dp", dp, pl.ds(0, O), ag2_sem)
+    ag2 = [
+        remote(dp.at[slot, rows, :], dp.at[slot, rows, :], ag2_sem.at[0, k], ag2_sem.at[1, k], at(q, c, to))
+        for k, (slot, first, count, to) in enumerate((
+            (y, 0, 1, up), (y, 2, 1, down), (y, 1, 1, up), (y, 3, 1, down), (y, 2, 2, up), (y, 0, 2, down),
+            (down, 0, 1, up), (up, 2, 1, down), (down, 1, 1, up), (up, 3, 1, down),
+        ))
+        for rows in [pl.ds(first * (N // 4), count * (N // 4))]
+    ]
+    for k in range(6):
+        started(f"dp{k}", ag2[k])
+
+    def forward_dp(k):
+        wait(f"dp{k}")
+        started(f"dp{k + 6}", ag2[k + 6])
+
     dT[...] = jnp.transpose(dp[y], (1, 0))
     turn_halo(far)
 
@@ -339,38 +366,38 @@
     put_terms(0, dot(tabT[:, 0:N], dp[y]))
     relation_terms(0)
     far_x(0)
+    pass_weights()
     relation_terms(1)
     far_x(1)
-    gather_forward("dp", ag2)
+    forward_dp(0)
+    forward_dp(1)
     near_x(0)
     for r in range(2, R):
         relation_terms(r)
         far_x(r)
+        if r == 2:
+            forward_dp(2)
+            forward_dp(3)
         near_x(r - 1)
     far_x(R)
-    forward_weights(1)
-    forward_weights(3)
     near_x(R - 1)
-    forward_weights(2)
 
     def own_back(r):
         bacc[r] = dot_nt(w[r, slot_rows(y), :], dp[y])
 
     def near_back(r):
-        bacc[r] += dot_nt(wd[down, r], dp[down]) + dot_nt(wd[up, r], dp[up])
+        bacc[r] += dot_nt(wd[0, r], dp[down]) + dot_nt(wd[2, r], dp[up])
 
     def far_back(r):
-        bT[r] = (bacc[r] + dot_nt(wd[far, r], dp[far])).astype(BF16)
+        bT[r] = (bacc[r] + dot_nt(wd[1, r], dp[far])).astype(BF16)
 
     loop(R + 1, own_back)
     near_x(R)
-    for k in (1, 3):
-        wait(f"wf{k}")
-    for k in (2, 3):
+    wait("wf")
+    for k in (4, 5):
         wait(f"dp{k}")
     loop(R + 1, near_back)
-    wait("wf2")
-    for k in (4, 5):
+    for k in (6, 7, 8, 9):
         wait(f"dp{k}")
     for r in range(R):
         far_back(r)
@@ -390,7 +417,7 @@
     pending["ret"] = ret_all.wait_recv
     pending["ret out"] = ret_all.wait_send
 
-    own = bacc[R] + dot_nt(wd[far, R], dp[far])
+    own = bacc[R] + dot_nt(wd[1, R], dp[far])
     for r in range(R):
         own = own + dot(bT[r], cnt[r, :, 0:N])
     grad[...] = jnp.transpose(own, (1, 0))
@@ -488,7 +515,7 @@
             pltpu.VMEM((HR, S), BF16),
             pltpu.VMEM((HR, S), BF16),
             pltpu.VMEM((Y, HR, S), BF16),
-            pltpu.VMEM((Y, R + 1, S, O), BF16),
+            pltpu.VMEM((Y - 1, R + 1, S, O), BF16),
             pltpu.VMEM((R, N, K), jnp.int32),
             pltpu.VMEM((R, N, T), BF16),
             pltpu.VMEM((R, T, O), BF16),
@@ -518,9 +545,10 @@
             dma((2,)),
             dma((2, HALVES)),
             dma((2, Y)),
-            dma((2, Y)),
+            dma((2, X)),
+            dma((2,)),
             dma((HALVES, 2, 6)),
-            dma((2, 6)),
+            dma((2, 10)),
             dma((2, R + 1)),
             dma((2, R + 1, 2)),
             dma((2, R + 1, 2)),

time: 73.4 us -> 73.3 us (level)
  no operation moved by 1% of the time
where the time goes in v5:
time: 73.3 us; the launch traced here: 73.2 us
  Pallas kernels  72.5 us (99%)
    pallas_call x1, Pallas kernels, shards(): pl.pallas_call(functools.partial(kernel, X, Z, Y), out_shape=(jax.ShapeDt...  70.7 us
    pallas_call x1, Pallas kernels, shards(): pl.pallas_call(hand_out, out_shape=tuple((jax.ShapeDtypeStruct(one.shape,...  1.87 us

profile of v5, /device:TPU:1, one launch (start us, length us, event | category | flops | bytes accessed | tf_op | source)
XLA Modules:
  0.0 73.2 jit_solution(8196963314302180107)
XLA Ops:
  0.6 70.7 %graph_layer.1 = (bf16[512,256]{1,0:T(8,128)(2,1)}, bf16[512,256]{1,0:T(8,128)(2,1)}, f32[5,16,256]{2,1,0:T(8,128)}) custom-call(bf16[512,1024]{1,0:T(8,128)(2,1)} %feat_in.1, f32[512,1024]{1,0:T(8,128)} %hist_in.1, bf16[5,1024,256]{2,1,0:T(8,128)(2,1)} %bitcast.6, bf16[512,256]{1,0:T(8,128)(2,1)} %cot_in.1, s32[8,64]{1,0:T(8,128)} %bitcast.8, ...), custom_call_target="tpu_custom_call" | custom-call | tf_op jit(solution)/shard_map/graph_layer/pallas_call | solution.py:494
  71.3 1.9 %hand_out.1 = (bf16[512,256]{1,0:T(8,128)(2,1)}, bf16[512,256]{1,0:T(8,128)(2,1)}, f32[5,16,256]{2,1,0:T(8,128)}) custom-call(bf16[512,256]{1,0:T(8,128)(2,1)} %get-tuple-element.9.refs_0_, bf16[512,256]{1,0:T(8,128)(2,1)} %get-tuple-element.10.refs_1_, f32[5,16,256]{2,1,0:T(8,128)} %get-tuple-element.11.refs_2_), custom_call_target="tpu_custom_call" | custom-call | tf_op jit(solution)/shard_map/hand_out/pallas_call | solution.py:571

commit v6 on v5

--- a/solution.py
+++ b/solution.py
@@ -31,8 +31,8 @@
     feat_in, hist_in, w_in, cot_in, send_in, nbr_in,
     out, gf, gw,
     feat, w, cot, nbr, sendT, tcol, sendcol, histv, src, asib, aown, arecv, slabs, halo, wd, nbrcol, cnt, tab, tacc, pre, tabT,
-    dp, dT, eT, bacc, gsend, gown, grecv, gx, relay, rx, gz, gzs, rz, bT, grad, owners, hg, ret, rets,
-    in_sem, sib_sem, halo_sem, w_sem, wx_sem, wf_sem, ag1_sem, ag2_sem, gc_sem, gr_sem, gx_sem, gz_sem, ret_sem, rsib_sem,
+    dp, dT, eT, bacc, gsend, gown, grecv, gx, relay, rx, gz, gzs, rz, lz, lzr, lsum, lx, lxr, bT, grad, owners, hg, ret, rets,
+    in_sem, sib_sem, halo_sem, w_sem, wx_sem, wf_sem, ag1_sem, ag2_sem, gc_sem, gr_sem, gx_sem, gz_sem, lz_sem, lx_sem, ret_sem, rsib_sem,
 ):
     N, D = feat.shape
     R = nbr.shape[0]
@@ -255,9 +255,9 @@
     wait("feat")
     gather_halo(0)
     loop(R, local_tab)
+    share_weights()
     gather_halo(1)
     gather_forward("halo0", gathers[0])
-    share_weights()
 
     local = dot(feat[...], w[R])
     for r in range(R):
@@ -363,24 +363,48 @@
             gx[p, part] = (gown[p, part] + relay[p, k].astype(F32)).astype(BF16)
             started(f"x{p}{k}", x_copy(p, k, gx.at[p, pl.ds(to * Z, Z)], to))
 
+    def far_z():
+        wait(f"core{R}")
+
+        def body(i):
+            chips = pl.ds(i * Z, Z)
+            total = gown[R, chips] + grecv[R, chips].astype(F32)
+            gown[R, chips] = total
+            lz[i] = total.astype(BF16)
+
+        loop(X, body)
+        for k in range(1, Z):
+            to = ring(z + k, Z)
+            sems = lz_sem.at[0, k], lz_sem.at[1, k]
+            started(f"lz{k}", remote(lz.at[:, to], lzr.at[k - 1], *sems, at(x * Z + to, c, y)))
+
+    def near_z():
+        for k in range(1, Z):
+            wait(f"lz{k}")
+
+        def body(i):
+            total = gown[R, i * Z + z]
+            for k in range(1, Z):
+                total = total + lzr[k - 1, i].astype(F32)
+            lsum[i] = total
+            lx[i] = total.astype(BF16)
+
+        loop(X, body)
+        for k in range(1, X):
+            to = ring(x + k, X)
+            sems = lx_sem.at[0, k], lx_sem.at[1, k]
+            started(f"lx{k}", remote(lx.at[to], lxr.at[k - 1], *sems, at(to * Z + z, c, y)))
+
     put_terms(0, dot(tabT[:, 0:N], dp[y]))
-    relation_terms(0)
-    far_x(0)
-    pass_weights()
-    relation_terms(1)
-    far_x(1)
+    for r in range(R):
+        relation_terms(r)
+        far_x(r)
     forward_dp(0)
     forward_dp(1)
-    near_x(0)
-    for r in range(2, R):
-        relation_terms(r)
-        far_x(r)
-        if r == 2:
-            forward_dp(2)
-            forward_dp(3)
-        near_x(r - 1)
-    far_x(R)
-    near_x(R - 1)
+    far_z()
+    forward_dp(2)
+    forward_dp(3)
+    pass_weights()
 
     def own_back(r):
         bacc[r] = dot_nt(w[r, slot_rows(y), :], dp[y])
@@ -391,8 +415,10 @@
     def far_back(r):
         bT[r] = (bacc[r] + dot_nt(wd[1, r], dp[far])).astype(BF16)
 
+    near_x(0)
     loop(R + 1, own_back)
-    near_x(R)
+    for p in range(1, R):
+        near_x(p)
     wait("wf")
     for k in (4, 5):
         wait(f"dp{k}")
@@ -417,11 +443,6 @@
     pending["ret"] = ret_all.wait_recv
     pending["ret out"] = ret_all.wait_send
 
-    own = bacc[R] + dot_nt(wd[1, R], dp[far])
-    for r in range(R):
-        own = own + dot(bT[r], cnt[r, :, 0:N])
-    grad[...] = jnp.transpose(own, (1, 0))
-
     def z_copy(g, places, k):
         to = ring(z + k, Z)
         return remote(
@@ -439,8 +460,13 @@
         for k in range(1, Z):
             started(f"z{g}{k}", z_copy(g, pl.ds(first, last - first), k))
 
-    first_group = (R + 2) // 2
+    first_group = R // 2
     along_z(0, 0, first_group)
+
+    own = bacc[R] + dot_nt(wd[1, R], dp[far])
+    for r in range(R):
+        own = own + dot(bT[r], cnt[r, :, 0:N])
+    grad[...] = jnp.transpose(own, (1, 0))
 
     def owner_map(k):
         rows = lax.broadcasted_iota(jnp.int32, (N, HR), 0)
@@ -449,7 +475,8 @@
 
     for k in range(2):
         owners[k] = owner_map(k)
-    along_z(1, first_group, R + 1)
+    near_z()
+    along_z(1, first_group, R)
 
     wait("ret")
     started("rets", remote(ret, rets, rsib_sem.at[0], rsib_sem.at[1], sibling))
@@ -467,7 +494,12 @@
         wait(f"z0{k}")
         wait(f"z1{k}")
     total_terms(0, R)
-    loop(R, lambda r: total_terms(r + 1, r))
+    loop(R - 1, lambda r: total_terms(r + 1, r))
+    last = lsum[x]
+    for k in range(1, X):
+        wait(f"lx{k}")
+        last = last + lxr[k - 1].astype(F32)
+    gw[R - 1] = last
     finish()
 
 
@@ -529,12 +561,17 @@
             pltpu.VMEM((R + 1, CH, GR, O), BF16),
             pltpu.VMEM((R + 1, CH, GR, O), F32),
             pltpu.VMEM((R + 1, CH, GR, O), BF16),
-            pltpu.VMEM((R + 1, CH, GR, O), BF16),
-            pltpu.VMEM((R + 1, 2, Z // 2, GR, O), BF16),
-            pltpu.VMEM((R + 1, 2, Z, GR, O), BF16),
-            pltpu.VMEM((R + 1, Z, GR, O), F32),
-            pltpu.VMEM((R + 1, Z, GR, O), BF16),
-            pltpu.VMEM((Z - 1, R + 1, GR, O), BF16),
+            pltpu.VMEM((R, CH, GR, O), BF16),
+            pltpu.VMEM((R, 2, Z // 2, GR, O), BF16),
+            pltpu.VMEM((R, 2, Z, GR, O), BF16),
+            pltpu.VMEM((R, Z, GR, O), F32),
+            pltpu.VMEM((R, Z, GR, O), BF16),
+            pltpu.VMEM((Z - 1, R, GR, O), BF16),
+            pltpu.VMEM((X, Z, GR, O), BF16),
+            pltpu.VMEM((Z - 1, X, GR, O), BF16),
+            pltpu.VMEM((X, GR, O), F32),
+            pltpu.VMEM((X, GR, O), BF16),
+            pltpu.VMEM((X - 1, GR, O), BF16),
             pltpu.VMEM((R, S, N), BF16),
             pltpu.VMEM((N, S), F32),
             pltpu.VMEM((2, N, HR), BF16),
@@ -550,9 +587,11 @@
             dma((HALVES, 2, 6)),
             dma((2, 10)),
             dma((2, R + 1)),
-            dma((2, R + 1, 2)),
-            dma((2, R + 1, 2)),
+            dma((2, R, 2)),
+            dma((2, R, 2)),
             dma((2, 2, Z)),
+            dma((2, Z)),
+            dma((2, X)),
             dma((2,)),
             dma((2,)),
         ],

time: 73.3 us -> 67.5 us (0.921)
  Pallas kernels: 72.5 us -> 66.7 us
    pallas_call x1, Pallas kernels: 70.7 us -> 64.9 us  [shards(): pl.pallas_call(functools.partial(kernel, X, Z, Y), out_shape=(jax.ShapeDt...]
where the time goes in v6:
time: 67.5 us; the launch traced here: 67.4 us
  Pallas kernels  66.7 us (99%)
    pallas_call x1, Pallas kernels, shards(): pl.pallas_call(functools.partial(kernel, X, Z, Y), out_shape=(jax.ShapeDt...  64.9 us
    pallas_call x1, Pallas kernels, shards(): pl.pallas_call(hand_out, out_shape=tuple((jax.ShapeDtypeStruct(one.shape,...  1.87 us

profile of v6, /device:TPU:1, one launch (start us, length us, event | category | flops | bytes accessed | tf_op | source)
XLA Modules:
  0.0 67.4 jit_solution(13952589957220960792)
XLA Ops:
  0.6 64.9 %graph_layer.1 = (bf16[512,256]{1,0:T(8,128)(2,1)}, bf16[512,256]{1,0:T(8,128)(2,1)}, f32[5,16,256]{2,1,0:T(8,128)}) custom-call(bf16[512,1024]{1,0:T(8,128)(2,1)} %feat_in.1, f32[512,1024]{1,0:T(8,128)} %hist_in.1, bf16[5,1024,256]{2,1,0:T(8,128)(2,1)} %bitcast.6, bf16[512,256]{1,0:T(8,128)(2,1)} %cot_in.1, s32[8,64]{1,0:T(8,128)} %bitcast.8, ...), custom_call_target="tpu_custom_call" | custom-call | tf_op jit(solution)/shard_map/graph_layer/pallas_call | solution.py:526
  65.5 1.9 %hand_out.1 = (bf16[512,256]{1,0:T(8,128)(2,1)}, bf16[512,256]{1,0:T(8,128)(2,1)}, f32[5,16,256]{2,1,0:T(8,128)}) custom-call(bf16[512,256]{1,0:T(8,128)(2,1)} %get-tuple-element.9.refs_0_, bf16[512,256]{1,0:T(8,128)(2,1)} %get-tuple-element.10.refs_1_, f32[5,16,256]{2,1,0:T(8,128)} %get-tuple-element.11.refs_2_), custom_call_target="tpu_custom_call" | custom-call | tf_op jit(solution)/shard_map/hand_out/pallas_call | solution.py:610

commit v7 on v6

--- a/solution.py
+++ b/solution.py
@@ -87,15 +87,20 @@
         ("send", send_in, sendT),
         ("feat slice", feat_in.at[:, columns], src.at[pl.ds(0, N), :]),
         ("hist", hist_in.at[:, columns], histv),
+        ("w", w_in, w),
         ("nbr", nbr_in, nbr),
         ("feat", feat_in, feat),
-        ("w", w_in, w),
         ("cot", cot_in, cot),
     ]
-    for i, (name, here, there) in enumerate(inputs):
-        cp = pltpu.make_async_copy(here, there, in_sem.at[i])
-        cp.start()
-        pending[name] = cp.wait
+
+    def fetch(first, last):
+        for i in range(first, last):
+            name, here, there = inputs[i]
+            cp = pltpu.make_async_copy(here, there, in_sem.at[i])
+            cp.start()
+            pending[name] = cp.wait
+
+    fetch(0, 3)
 
     barrier = pltpu.get_barrier_semaphore()
 
@@ -119,6 +124,7 @@
         sendcol[k] = found.reshape(HR, 1).astype(jnp.int32)
     wait("feat slice")
     wait("hist")
+    fetch(3, len(inputs))
     src[N : 2 * N, :] = histv[...].astype(BF16)
 
     def pick(k, dst):
@@ -162,10 +168,6 @@
         part = wd.at[:, :, half_rows, :]
         started("wf", remote(part, part, wf_sem.at[0], wf_sem.at[1], sibling))
 
-    wait("w")
-    send_weights(1)
-    send_weights(3)
-    send_weights(2)
     started("sib", remote(asib, arecv, sib_sem.at[0], sib_sem.at[1], sibling))
     pick(0, aown)
     wait("sib")
@@ -173,23 +175,36 @@
     mine = pl.ds(pl.multiple_of(q * SL, SL), SL)
     halo[y, mine, :] = slabs[mine, :]
 
-    def chip_rows(i):
-        chip = lax.rem(q + 1 + i, CH)
-        return chip, pl.ds(pl.multiple_of(chip * SL, SL), SL)
+    def other_chips(body):
+        for dz in sorted(range(Z), key=lambda d: -min(d, Z - d)):
+
+            def along(i):
+                chip = ring(x + X // 2 + i, X) * Z + ring(z + dz, Z)
+                body(chip, pl.ds(pl.multiple_of(chip * SL, SL), SL))
+
+            if dz:
+                loop(X, along)
+            else:
+                for i in range(X):
+                    if i != X // 2:
+                        along(i)
 
     others = pl.ds(0, HR - SL)
     part_cols = [pl.ds(h * (S // HALVES), S // HALVES) for h in range(HALVES)]
     for h, cols in enumerate(part_cols):
         sems = halo_sem.at[0, h], halo_sem.at[1, h]
 
-        def send_slab(i):
-            chip, rows = chip_rows(i)
+        def send_slab(chip, rows):
             remote(slabs.at[rows, cols], halo.at[y, mine, cols], *sems, at(chip, c, y)).start()
 
-        loop(CH - 1, send_slab)
+        other_chips(send_slab)
         everything = remote(slabs.at[others, cols], halo.at[y, others, cols], *sems, sibling)
         pending[f"slabs{h}"] = everything.wait_recv
         pending[f"slabs{h} out"] = everything.wait_send
+
+    wait("w")
+    for k in (2, 1, 3):
+        send_weights(k)
 
     wait("nbr")
 
@@ -363,47 +378,53 @@
             gx[p, part] = (gown[p, part] + relay[p, k].astype(F32)).astype(BF16)
             started(f"x{p}{k}", x_copy(p, k, gx.at[p, pl.ds(to * Z, Z)], to))
 
-    def far_z():
-        wait(f"core{R}")
+    z_first = (0, R)
+
+    def far_z(l):
+        p = z_first[l]
+        wait(f"core{p}")
 
         def body(i):
             chips = pl.ds(i * Z, Z)
-            total = gown[R, chips] + grecv[R, chips].astype(F32)
-            gown[R, chips] = total
-            lz[i] = total.astype(BF16)
+            total = gown[p, chips] + grecv[p, chips].astype(F32)
+            gown[p, chips] = total
+            lz[l, i] = total.astype(BF16)
 
         loop(X, body)
         for k in range(1, Z):
             to = ring(z + k, Z)
-            sems = lz_sem.at[0, k], lz_sem.at[1, k]
-            started(f"lz{k}", remote(lz.at[:, to], lzr.at[k - 1], *sems, at(x * Z + to, c, y)))
-
-    def near_z():
+            sems = lz_sem.at[l, 0, k], lz_sem.at[l, 1, k]
+            started(f"lz{l}{k}", remote(lz.at[l, :, to], lzr.at[l, k - 1], *sems, at(x * Z + to, c, y)))
+
+    def near_z(l):
         for k in range(1, Z):
-            wait(f"lz{k}")
+            wait(f"lz{l}{k}")
 
         def body(i):
-            total = gown[R, i * Z + z]
+            total = gown[z_first[l], i * Z + z]
             for k in range(1, Z):
-                total = total + lzr[k - 1, i].astype(F32)
-            lsum[i] = total
-            lx[i] = total.astype(BF16)
+                total = total + lzr[l, k - 1, i].astype(F32)
+            lsum[l, i] = total
+            lx[l, i] = total.astype(BF16)
 
         loop(X, body)
         for k in range(1, X):
             to = ring(x + k, X)
-            sems = lx_sem.at[0, k], lx_sem.at[1, k]
-            started(f"lx{k}", remote(lx.at[to], lxr.at[k - 1], *sems, at(to * Z + z, c, y)))
+            sems = lx_sem.at[l, 0, k], lx_sem.at[l, 1, k]
+            started(f"lx{l}{k}", remote(lx.at[l, to], lxr.at[l, k - 1], *sems, at(to * Z + z, c, y)))
 
     put_terms(0, dot(tabT[:, 0:N], dp[y]))
-    for r in range(R):
+    relation_terms(0)
+    far_z(0)
+    for r in range(1, R):
         relation_terms(r)
         far_x(r)
-    forward_dp(0)
-    forward_dp(1)
-    far_z()
+        if r == R - 2:
+            forward_dp(0)
+            forward_dp(1)
     forward_dp(2)
     forward_dp(3)
+    far_z(1)
     pass_weights()
 
     def own_back(r):
@@ -415,7 +436,6 @@
     def far_back(r):
         bT[r] = (bacc[r] + dot_nt(wd[1, r], dp[far])).astype(BF16)
 
-    near_x(0)
     loop(R + 1, own_back)
     for p in range(1, R):
         near_x(p)
@@ -434,11 +454,10 @@
     hg[...] = jnp.transpose(received, (1, 0)).astype(BF16)
     ret[mine, :] = hg[mine, :]
 
-    def return_slab(i):
-        chip, rows = chip_rows(i)
+    def return_slab(chip, rows):
         remote(hg.at[rows, :], ret.at[mine, :], ret_sem.at[0], ret_sem.at[1], at(chip, c, y)).start()
 
-    loop(CH - 1, return_slab)
+    other_chips(return_slab)
     ret_all = remote(hg.at[others, :], ret.at[others, :], ret_sem.at[0], ret_sem.at[1], sibling)
     pending["ret"] = ret_all.wait_recv
     pending["ret out"] = ret_all.wait_send
@@ -460,8 +479,8 @@
         for k in range(1, Z):
             started(f"z{g}{k}", z_copy(g, pl.ds(first, last - first), k))
 
-    first_group = R // 2
-    along_z(0, 0, first_group)
+    near_z(0)
+    along_z(0, 1, R - 1)
 
     own = bacc[R] + dot_nt(wd[1, R], dp[far])
     for r in range(R):
@@ -475,8 +494,8 @@
 
     for k in range(2):
         owners[k] = owner_map(k)
-    near_z()
-    along_z(1, first_group, R)
+    near_z(1)
+    along_z(1, R - 1, R)
 
     wait("ret")
     started("rets", remote(ret, rets, rsib_sem.at[0], rsib_sem.at[1], sibling))
@@ -493,13 +512,13 @@
     for k in range(1, Z):
         wait(f"z0{k}")
         wait(f"z1{k}")
-    total_terms(0, R)
     loop(R - 1, lambda r: total_terms(r + 1, r))
-    last = lsum[x]
-    for k in range(1, X):
-        wait(f"lx{k}")
-        last = last + lxr[k - 1].astype(F32)
-    gw[R - 1] = last
+    for l, r in enumerate((R, R - 1)):
+        last = lsum[l, x]
+        for k in range(1, X):
+            wait(f"lx{l}{k}")
+            last = last + lxr[l, k - 1].astype(F32)
+        gw[r] = last
     finish()
 
 
@@ -567,11 +586,11 @@
             pltpu.VMEM((R, Z, GR, O), F32),
             pltpu.VMEM((R, Z, GR, O), BF16),
             pltpu.VMEM((Z - 1, R, GR, O), BF16),
-            pltpu.VMEM((X, Z, GR, O), BF16),
-            pltpu.VMEM((Z - 1, X, GR, O), BF16),
-            pltpu.VMEM((X, GR, O), F32),
-            pltpu.VMEM((X, GR, O), BF16),
-            pltpu.VMEM((X - 1, GR, O), BF16),
+            pltpu.VMEM((2, X, Z, GR, O), BF16),
+            pltpu.VMEM((2, Z - 1, X, GR, O), BF16),
+            pltpu.VMEM((2, X, GR, O), F32),
+            pltpu.VMEM((2, X, GR, O), BF16),
+            pltpu.VMEM((2, X - 1, GR, O), BF16),
             pltpu.VMEM((R, S, N), BF16),
             pltpu.VMEM((N, S), F32),
             pltpu.VMEM((2, N, HR), BF16),
@@ -590,8 +609,8 @@
             dma((2, R, 2)),
             dma((2, R, 2)),
             dma((2, 2, Z)),
-            dma((2, Z)),
-            dma((2, X)),
+            dma((2, 2, Z)),
+            dma((2, 2, X)),
             dma((2,)),
             dma((2,)),
         ],

time: 67.5 us -> 65.5 us (0.970)
  Pallas kernels: 66.7 us -> 64.7 us
    pallas_call x1, Pallas kernels: 64.9 us -> 62.8 us  [shards(): pl.pallas_call(functools.partial(kernel, X, Z, Y), out_shape=(jax.ShapeDt...]
where the time goes in v7:
time: 65.5 us; the launch traced here: 65.4 us
  Pallas kernels  64.7 us (99%)
    pallas_call x1, Pallas kernels, shards(): pl.pallas_call(functools.partial(kernel, X, Z, Y), out_shape=(jax.ShapeDt...  62.8 us
    pallas_call x1, Pallas kernels, shards(): pl.pallas_call(hand_out, out_shape=tuple((jax.ShapeDtypeStruct(one.shape,...  1.87 us

profile of v7, /device:TPU:1, one launch (start us, length us, event | category | flops | bytes accessed | tf_op | source)
XLA Modules:
  0.0 65.4 jit_solution(14974139542319933766)
XLA Ops:
  0.6 62.8 %graph_layer.1 = (bf16[512,256]{1,0:T(8,128)(2,1)}, bf16[512,256]{1,0:T(8,128)(2,1)}, f32[5,16,256]{2,1,0:T(8,128)}) custom-call(bf16[512,1024]{1,0:T(8,128)(2,1)} %feat_in.1, f32[512,1024]{1,0:T(8,128)} %hist_in.1, bf16[5,1024,256]{2,1,0:T(8,128)(2,1)} %bitcast.6, bf16[512,256]{1,0:T(8,128)(2,1)} %cot_in.1, s32[8,64]{1,0:T(8,128)} %bitcast.8, ...), custom_call_target="tpu_custom_call" | custom-call | tf_op jit(solution)/shard_map/graph_layer/pallas_call | solution.py:545
  63.5 1.9 %hand_out.1 = (bf16[512,256]{1,0:T(8,128)(2,1)}, bf16[512,256]{1,0:T(8,128)(2,1)}, f32[5,16,256]{2,1,0:T(8,128)}) custom-call(bf16[512,256]{1,0:T(8,128)(2,1)} %get-tuple-element.9.refs_0_, bf16[512,256]{1,0:T(8,128)(2,1)} %get-tuple-element.10.refs_1_, f32[5,16,256]{2,1,0:T(8,128)} %get-tuple-element.11.refs_2_), custom_call_target="tpu_custom_call" | custom-call | tf_op jit(solution)/shard_map/hand_out/pallas_call | solution.py:629

commit v8 on v7

--- a/solution.py
+++ b/solution.py
@@ -107,10 +107,24 @@
     def greet(dev):
         pl.semaphore_signal(barrier, inc=1, device_id=dev, device_id_type=MESH)
 
+    def other_chips(body):
+        for dz in sorted(range(Z), key=lambda d: -min(d, Z - d)):
+
+            def along(i):
+                chip = ring(x + X // 2 + i, X) * Z + ring(z + dz, Z)
+                body(chip, pl.ds(pl.multiple_of(chip * SL, SL), SL))
+
+            if dz:
+                loop(X, along)
+            else:
+                for i in range(X):
+                    if i != X // 2:
+                        along(i)
+
+    other_chips(lambda chip, rows: greet(at(chip, c, y)))
     greet(sibling)
     for k in range(1, Y):
         greet(at(q, c, ring(y + k, Y)))
-    loop(CH - 1, lambda i: greet(at(lax.rem(q + 1 + i, CH), c, y)))
 
     wait("send")
     tcol[...] = jnp.transpose(sendT[...].astype(F32), (1, 0))
@@ -175,20 +189,6 @@
     mine = pl.ds(pl.multiple_of(q * SL, SL), SL)
     halo[y, mine, :] = slabs[mine, :]
 
-    def other_chips(body):
-        for dz in sorted(range(Z), key=lambda d: -min(d, Z - d)):
-
-            def along(i):
-                chip = ring(x + X // 2 + i, X) * Z + ring(z + dz, Z)
-                body(chip, pl.ds(pl.multiple_of(chip * SL, SL), SL))
-
-            if dz:
-                loop(X, along)
-            else:
-                for i in range(X):
-                    if i != X // 2:
-                        along(i)
-
     others = pl.ds(0, HR - SL)
     part_cols = [pl.ds(h * (S // HALVES), S // HALVES) for h in range(HALVES)]
     for h, cols in enumerate(part_cols):
@@ -492,11 +492,13 @@
         named = jnp.transpose(jnp.broadcast_to(sendcol[k], (HR, 8)), (1, 0))[0:1]
         return jnp.where(named == rows, 1.0, 0.0).astype(BF16)
 
+    near_z(1)
+    along_z(1, R - 1, R)
     for k in range(2):
         owners[k] = owner_map(k)
-    near_z(1)
-    along_z(1, R - 1, R)
-
+
+    for name in [name for name in pending if name.endswith(" out") and not name.startswith(("ret", "z", "l"))]:
+        wait(name)
     wait("ret")
     started("rets", remote(ret, rets, rsib_sem.at[0], rsib_sem.at[1], sibling))
     grad[...] += dot(owners[0], ret[...])

time: 65.5 us -> 65.2 us (level)
  no operation moved by 1% of the time
where the time goes in v8:
time: 65.2 us; the launch traced here: 65 us
  Pallas kernels  64.4 us (99%)
    pallas_call x1, Pallas kernels, shards(): pl.pallas_call(functools.partial(kernel, X, Z, Y), out_shape=(jax.ShapeDt...  62.5 us
    pallas_call x1, Pallas kernels, shards(): pl.pallas_call(hand_out, out_shape=tuple((jax.ShapeDtypeStruct(one.shape,...  1.87 us

profile of v8, /device:TPU:1, one launch (start us, length us, event | category | flops | bytes accessed | tf_op | source)
XLA Modules:
  0.0 65.0 jit_solution(3588751035461925615)
XLA Ops:
  0.6 62.5 %graph_layer.1 = (bf16[512,256]{1,0:T(8,128)(2,1)}, bf16[512,256]{1,0:T(8,128)(2,1)}, f32[5,16,256]{2,1,0:T(8,128)}) custom-call(bf16[512,1024]{1,0:T(8,128)(2,1)} %feat_in.1, f32[512,1024]{1,0:T(8,128)} %hist_in.1, bf16[5,1024,256]{2,1,0:T(8,128)(2,1)} %bitcast.6, bf16[512,256]{1,0:T(8,128)(2,1)} %cot_in.1, s32[8,64]{1,0:T(8,128)} %bitcast.8, ...), custom_call_target="tpu_custom_call" | custom-call | tf_op jit(solution)/shard_map/graph_layer/pallas_call | solution.py:547
  63.2 1.9 %hand_out.1 = (bf16[512,256]{1,0:T(8,128)(2,1)}, bf16[512,256]{1,0:T(8,128)(2,1)}, f32[5,16,256]{2,1,0:T(8,128)}) custom-call(bf16[512,256]{1,0:T(8,128)(2,1)} %get-tuple-element.9.refs_0_, bf16[512,256]{1,0:T(8,128)(2,1)} %get-tuple-element.10.refs_1_, f32[5,16,256]{2,1,0:T(8,128)} %get-tuple-element.11.refs_2_), custom_call_target="tpu_custom_call" | custom-call | tf_op jit(solution)/shard_map/hand_out/pallas_call | solution.py:631
